TPU v7x, 512 devices: a whole 4x4x16 slice. The times are simulated.
512 devices in a mesh: seq: 32 (over y, x, core), head: 16 (over z).
Axes of the slice: x: 4, y: 4, z: 16, core: 2. Of those that a mesh axis runs over, the one named last changes fastest.
Arguments:
- queries: bfloat16 [256, 128, 192], P('seq', 'head'), may hold values from -260 to 260
- prompt_cache: bfloat16 [32768, 576], P('seq'), may hold values from -8 to 8
- suffix_cache: bfloat16 [64, 256, 576], P('seq'), may hold values from -6 to 6
- gen_lengths: int32 [64], P('seq'), may hold values from 1 to 256
- new_latent: bfloat16 [256, 512], P('seq', 'head'), may hold values from -24 to 24
- new_rope: bfloat16 [256, 64], P('seq'), may hold values from -6 to 6
- latent_gain: bfloat16 [512], P('head'), may hold values from 0.25 to 1.75
- w_uk: bfloat16 [128, 128, 512], P('head'), may hold values from -0.5 to 0.5
- w_uv: bfloat16 [128, 512, 128], P('head'), may hold values from -0.25 to 0.25
Outputs:
- attn_values: bfloat16 [256, 16384], P('seq', 'head')
All inputs are finite; a program needn't handle non-finite values.
Results may differ from a plain program's by a relative error of at most 0.0075.
Values may be sent and summed in bfloat16 or wider, within the bound.
No kernel may reach another device: no remote copies, remote signals or barrier semaphores. Data moves between devices by JAX's collectives and lax.ppermute only.
A program may use at most 64 MiB of HBM per device.

v0:
```python
import jax
import jax.numpy as jnp
from jax import lax
from jax.sharding import PartitionSpec as P

eps = 1e-06


def per_device(
    queries, prompt_cache, suffix_cache, gen_lengths, new_latent, new_rope, latent_gain, w_uk, w_uv
):
    nope = w_uk.shape[1]
    latent = w_uk.shape[2]
    local_rows, local_heads, width = queries.shape
    key_width = prompt_cache.shape[1]
    samples_here = suffix_cache.shape[0]
    steps_here = local_rows // samples_here
    gen_most = suffix_cache.shape[1]
    scale = float(width) ** (-0.5)
    plain = new_latent.astype(jnp.float32)
    squared = lax.psum(jnp.sum(plain * plain, -1), "head")
    scaled = (
        plain * lax.rsqrt(squared[:, None] / latent + eps) * latent_gain.astype(jnp.float32)
    ).astype(jnp.bfloat16)
    normed = lax.all_gather(scaled, "head", axis=1, tiled=True)
    absorbed = jnp.einsum(
        "qhn,hnl->qhl", queries[:, :, :nope], w_uk, preferred_element_type=jnp.float32
    ).astype(jnp.bfloat16)
    mine = jnp.concatenate([absorbed, queries[:, :, nope:]], -1)
    every = lax.all_gather(mine, "seq", axis=0, tiled=True)
    total_rows = every.shape[0]
    flat = every.reshape(total_rows * local_heads, key_width)
    block = min(512, prompt_cache.shape[0])
    blocks = prompt_cache.reshape(prompt_cache.shape[0] // block, block, key_width)

    def visit(carry, keys):
        accum, peak_now, mass = carry
        scores = (
            lax.dot_general(
                flat, keys, (((1,), (1,)), ((), ())), preferred_element_type=jnp.float32
            )
            * scale
        )
        peak_new = jnp.maximum(peak_now, jnp.max(scores, -1))
        fade = jnp.exp(peak_now - peak_new)
        expd = jnp.exp(scores - peak_new[:, None])
        mass = mass * fade + jnp.sum(expd, -1)
        accum = accum * fade[:, None] + jnp.dot(
            expd.astype(jnp.bfloat16), keys[:, :latent], preferred_element_type=jnp.float32
        )
        return ((accum, peak_new, mass), None)

    count_all = total_rows * local_heads
    start = (
        jnp.zeros((count_all, latent), jnp.float32),
        jnp.full((count_all,), -jnp.inf, jnp.float32),
        jnp.zeros((count_all,), jnp.float32),
    )
    (accum, peak_now, mass), _ = lax.scan(visit, start, blocks)
    accum = accum.reshape(total_rows, local_heads, latent)
    peak_now = peak_now.reshape(total_rows, local_heads)
    mass = mass.reshape(total_rows, local_heads)
    width_seq = lax.axis_size("seq")
    parts = (
        lax.all_to_all(
            accum.reshape(width_seq, local_rows, local_heads, latent),
            "seq",
            split_axis=0,
            concat_axis=0,
            tiled=True,
        ),
        lax.all_to_all(
            peak_now.reshape(width_seq, local_rows, local_heads),
            "seq",
            split_axis=0,
            concat_axis=0,
            tiled=True,
        ),
        lax.all_to_all(
            mass.reshape(width_seq, local_rows, local_heads),
            "seq",
            split_axis=0,
            concat_axis=0,
            tiled=True,
        ),
    )
    peak_all = jnp.max(parts[1], 0)
    fade = jnp.exp(parts[1] - peak_all[None])
    accum = jnp.sum(parts[0] * fade[..., None], 0)
    mass = jnp.sum(parts[2] * fade, 0)
    peak_now = peak_all
    grouped = mine.reshape(samples_here, steps_here, local_heads, key_width)
    suffix_scores = (
        jnp.einsum("bthc,bgc->bthg", grouped, suffix_cache, preferred_element_type=jnp.float32)
        * scale
    )
    live = (jnp.arange(gen_most)[None, :] < gen_lengths[:, None])[:, None, None, :]
    suffix_scores = jnp.where(live, suffix_scores, -jnp.inf)
    fresh_keys = jnp.concatenate([normed, new_rope], -1).reshape(
        samples_here, steps_here, key_width
    )
    fresh_scores = (
        jnp.einsum("bthc,buc->bthu", grouped, fresh_keys, preferred_element_type=jnp.float32)
        * scale
    )
    causal = (jnp.arange(steps_here)[None, :] <= jnp.arange(steps_here)[:, None])[None, :, None, :]
    fresh_scores = jnp.where(causal, fresh_scores, -jnp.inf)
    prior_peak = peak_now.reshape(samples_here, steps_here, local_heads)
    prior_mass = mass.reshape(samples_here, steps_here, local_heads)
    prior_acc = accum.reshape(samples_here, steps_here, local_heads, latent)
    peak = jnp.maximum(
        prior_peak, jnp.maximum(jnp.max(suffix_scores, -1), jnp.max(fresh_scores, -1))
    )
    fade = jnp.exp(prior_peak - peak)
    suffix_exp = jnp.exp(suffix_scores - peak[..., None])
    fresh_exp = jnp.exp(fresh_scores - peak[..., None])
    total = prior_mass * fade + jnp.sum(suffix_exp, -1) + jnp.sum(fresh_exp, -1)
    summed = prior_acc * fade[..., None]
    summed = summed + jnp.einsum(
        "bthg,bgl->bthl",
        suffix_exp.astype(jnp.bfloat16),
        suffix_cache[:, :, :latent],
        preferred_element_type=jnp.float32,
    )
    summed = summed + jnp.einsum(
        "bthu,bul->bthl",
        fresh_exp.astype(jnp.bfloat16),
        fresh_keys[:, :, :latent],
        preferred_element_type=jnp.float32,
    )
    attn_latent = (
        (summed / total[..., None]).astype(jnp.bfloat16).reshape(local_rows, local_heads, latent)
    )
    result = jnp.einsum(
        "qhl,hlv->qhv", attn_latent, w_uv, preferred_element_type=jnp.float32
    ).astype(jnp.bfloat16)
    return result.reshape(local_rows, local_heads * w_uv.shape[2])


def solution(mesh):
    return jax.shard_map(
        per_device,
        mesh=mesh,
        in_specs=(
            P("seq", "head", None),
            P("seq", None),
            P("seq", None, None),
            P("seq"),
            P("seq", "head"),
            P("seq", None),
            P("head"),
            P("head", None, None),
            P("head", None, None),
        ),
        out_specs=P("seq", "head"),
        check_vma=False,
    )
```

profile of v0, /device:TPU:6, one launch (start us, length us, event | category | flops | bytes accessed | tf_op | source)
XLA Modules:
  0.0 206.8 jit_solution(1932800585279150658)
XLA Ops:
  6.5 0.0 copy-start
  6.5 0.0 all-gather.3.cloned.1.call-start
  6.5 0.8 slice.15
  7.3 0.7 slice.16
  8.1 0.0 copy-done
  8.1 0.2 fusion.12
  8.3 0.7 pad_maximum_fusion
  9.0 0.0 all-gather.3.cloned.1.call-update
  9.0 1.7 copy.53
  10.7 63.6 %all-gather.3.cloned.1.call-done = bf16[256,8,576]{2,0,1:T(8,128)(2,1)} async-done(((bf16[8,8,576]{2,0,1:T(8,128)(2,1)}), bf16[256,8,576]{2,0,1:T(8,128)(2,1)}) %all-gather.3.cloned.1.call-update) | async-done | bytes 2359312 | tf_op jit(solution)/shard_map/all_gather | solution.py:30
  74.3 4.8 %copy.86 = bf16[256,8,576]{2,1,0:T(8,128)(2,1)} copy(bf16[256,8,576]{2,0,1:T(8,128)(2,1)} %all-gather.3.cloned.1.call-done) | data formatting | bytes 4718592 | tf_op jit(solution)/shard_map/all_gather | solution.py:30
  79.1 25.4 %while.15 = (s32[]{:T(128)}, f32[2048,512]{1,0:T(8,128)}, f32[2048]{0:T(1024)S(1)}, f32[2048]{0:T(1024)S(1)}, bf16[2,512,576]{2,1,0:T(8,128)(2,1)S(1)}, /*index=5*/bf16[2048,576]{1,0:T(8,128)(2,1)}, s32[]{:T(128)}, s32[]{:T(128)}) while((s32[]{:T(128)}, f32[2048,512]{1,0:T(8,128)}, f32[2048]{0:T(1024)S(1)}, f32[2048]{0:T(1024)S(1)}, ...), condition=%wide.region_3.0_spmd.clone, body=%wide.region_0.3_spmd.clone.sunk | while | flops 2293245952 | bytes 42532988 | solution.py:59
  79.1 0.1 dynamic-slice_bitcast_fusion.2
  79.2 5.5 %multiply_reduce_fusion.4 = (f32[2048]{0:T(1024)S(1)}, f32[512,2048]{1,0:T(8,128)}) fusion(bf16[512,576]{1,0:T(8,128)(2,1)S(1)} %dynamic-slice_bitcast_fusion.2, bf16[2048,576]{1,0:T(8,128)(2,1)} %get-tuple-element.157), kind=kOutput, calls=%fused_computation.3.clone.1 | convolution fusion | flops 1210054656 | bytes 7151616 | tf_op jit(solution)/shard_map/while/body/eval_jaxpr/dot_general | solution.py:39
  84.8 0.0 copy-start.1
  84.8 3.0 %fusion.53 = f32[2048]{0:T(1024)S(1)} fusion(f32[512,2048]{1,0:T(8,128)} %get-tuple-element.132, f32[2048]{0:T(1024)S(1)} %select_maximum_fusion.2), kind=kLoop, calls=%fused_computation.4.clone.1 | loop fusion | flops 3143680 | bytes 4210688 | tf_op jit(solution)/shard_map/while/body/eval_jaxpr/reduce_sum | solution.py:47
  87.8 0.4 copy-done.1
  88.2 2.8 %fusion.55 = f32[2048,512]{1,0:T(8,128)} fusion(f32[2048,512]{1,0:T(8,128)} %get-tuple-element.145, f32[512,2048]{1,0:T(8,128)S(1)} %copy-done.1, f32[2048]{0:T(1024)S(1)} %select_maximum_fusion.2, f32[2048]{0:T(1024)S(1)} %get-tuple-element.134, pred[]{:T(512)S(6)} %compare.3, bf16[512,576]{1,0:T(8,128)(2,1)S(1)} %dynamic-slice_bitcast_fusion.2), kind=kOutput, calls=%fused_computation.1.clone.1 | convolution fusion | flops 1080033280 | bytes 13123585 | tf_op jit(solution)/shard_map/while/body/eval_jaxpr/dot_general | solution.py:48
  91.0 0.1 dynamic-slice_bitcast_fusion.2
  91.1 5.5 %multiply_reduce_fusion.4 = (f32[2048]{0:T(1024)S(1)}, f32[512,2048]{1,0:T(8,128)}) fusion(bf16[512,576]{1,0:T(8,128)(2,1)S(1)} %dynamic-slice_bitcast_fusion.2, bf16[2048,576]{1,0:T(8,128)(2,1)} %get-tuple-element.157), kind=kOutput, calls=%fused_computation.3.clone.1 | convolution fusion | flops 1210054656 | bytes 7151616 | tf_op jit(solution)/shard_map/while/body/eval_jaxpr/dot_general | solution.py:39
  96.6 0.0 copy-start.1
  96.6 3.0 %fusion.53 = f32[2048]{0:T(1024)S(1)} fusion(f32[512,2048]{1,0:T(8,128)} %get-tuple-element.132, f32[2048]{0:T(1024)S(1)} %select_maximum_fusion.2), kind=kLoop, calls=%fused_computation.4.clone.1 | loop fusion | flops 3143680 | bytes 4210688 | tf_op jit(solution)/shard_map/while/body/eval_jaxpr/reduce_sum | solution.py:47
  99.7 0.4 copy-done.1
  100.1 4.4 %fusion.55 = f32[2048,512]{1,0:T(8,128)} fusion(f32[2048,512]{1,0:T(8,128)} %get-tuple-element.145, f32[512,2048]{1,0:T(8,128)S(1)} %copy-done.1, f32[2048]{0:T(1024)S(1)} %select_maximum_fusion.2, f32[2048]{0:T(1024)S(1)} %get-tuple-element.134, pred[]{:T(512)S(6)} %compare.3, bf16[512,576]{1,0:T(8,128)(2,1)S(1)} %dynamic-slice_bitcast_fusion.2), kind=kOutput, calls=%fused_computation.1.clone.1 | convolution fusion | flops 1080033280 | bytes 13123585 | tf_op jit(solution)/shard_map/while/body/eval_jaxpr/dot_general | solution.py:48
  104.5 0.7 reshape_reshape.10
  105.3 5.9 %all-to-all-start.1 = ((f32[32,8,8]{2,1,0:T(8,128)}), f32[32,8,8]{2,1,0:T(8,128)S(1)}, u32[]{:S(2)}, u32[]{:S(2)}) async-start(f32[32,8,8]{2,1,0:T(8,128)} %reshape_reshape.10), calls=%async_computation.1 | async-start | bytes 262144 | tf_op jit(solution)/shard_map/all_to_all | solution.py:72
  111.1 0.1 reshape_reshape.11
  111.2 6.0 %all-to-all-done.1 = f32[32,8,8]{2,1,0:T(8,128)S(1)} async-done(((f32[32,8,8]{2,1,0:T(8,128)}), f32[32,8,8]{2,1,0:T(8,128)S(1)}, u32[]{:S(2)}, u32[]{:S(2)}) %all-to-all-start.1) | async-done | bytes 8224 | tf_op jit(solution)/shard_map/all_to_all | solution.py:72
  117.2 11.3 %all_to_all.15 = f32[32,8,8]{2,1,0:T(8,128)S(1)} all-to-all(f32[32,8,8]{2,1,0:T(8,128)S(1)} %reshape_reshape.11), channel_id=1, replica_groups=mesh['seq'=32,'head'=16] {'seq'}, dimensions={0} | all-to-all | bytes 16384 | tf_op jit(solution)/shard_map/all_to_all | solution.py:79
  128.5 0.0 copy-start.5
  128.5 0.0 copy-start.3
  128.5 0.0 copy-start.7
  128.5 0.0 copy-start.6
  128.5 0.0 copy-start.8
  128.5 0.0 copy-start.4
  128.5 6.6 %all-to-all-start = ((f32[32,8,8,512]{3,2,1,0:T(8,128)}), f32[32,8,8,512]{3,2,1,0:T(8,128)}, u32[]{:S(2)}, u32[]{:S(2)}) async-start(f32[32,8,8,512]{3,2,1,0:T(8,128)} %bitcast.71), calls=%async_computation | async-start | bytes 8388608 | tf_op jit(solution)/shard_map/all_to_all | solution.py:65
  135.1 0.0 copy-done.5
  135.1 0.0 copy-start.2
  135.1 0.1 fusion.31
  135.2 31.4 %psum.7 = f32[8]{0:T(128)S(1)} all-reduce(f32[8]{0:T(128)S(1)} %fusion.31), channel_id=1, replica_groups=mesh['seq'=32,'head'=16] {'head'}, use_global_device_ids=true, to_apply=%region_8.9 | all-reduce | flops 8 | bytes 64 | tf_op jit(solution)/shard_map/psum | solution.py:21
  166.6 0.0 copy-done.3
  166.7 0.0 copy-done.7
  166.7 0.1 fusion.34
  166.8 27.4 %all-gather = bf16[16,32,8]{1,2,0:T(8,128)(2,1)S(1)} all-gather(bf16[1,32,8]{1,2,0:T(8,128)(2,1)S(1)} %fusion.34), channel_id=1, replica_groups=mesh['seq'=32,'head'=16] {'head'}, dimensions={0}, use_global_device_ids=true | all-gather | bytes 8704 | tf_op jit(solution)/shard_map/all_gather | solution.py:25
  194.2 0.1 reshape.117
  194.3 0.0 copy-done.6
  194.4 0.6 fusion.36
  194.9 0.1 copy.60
  195.0 0.0 copy-done.8
  195.0 0.1 iota_compare_fusion.1
  195.1 0.0 copy-done.4
  195.1 0.3 fusion.35
  195.5 0.1 copy.62
  195.6 0.1 copy.64
  195.7 0.1 copy.63
  195.8 0.2 fusion.22
  196.1 0.2 fusion.30
  196.3 0.0 all-to-all-done
  196.3 2.5 %multiply_reduce_fusion.1 = f32[8,8,512]{2,1,0:T(8,128)S(1)} fusion(f32[32,8,8,512]{3,2,1,0:T(8,128)} %all-to-all-done, f32[32,8,8]{2,1,0:T(8,128)S(1)} %get-tuple-element.80), kind=kLoop, calls=%fused_computation.15 | loop fusion | flops 2064384 | bytes 4333568 | tf_op jit(solution)/shard_map/reduce_sum | solution.py:89
  198.8 0.3 fusion.11
  199.1 0.0 copy-done.2
  199.1 0.9 fusion.15
  (23 shorter events, 0.3 us)
Async XLA Ops:
  6.5 1.5 copy-start
  6.5 67.8 %all-gather.3.cloned.1.call-start = ((), (), s32[]{:S(2)}) async-start(), calls=%async_computation.3 | async-start | bytes 2703360 | tf_op jit(solution)/shard_map/all_gather | solution.py:30
  84.8 3.4 %copy-start.1 = (f32[512,2048]{1,0:T(8,128)S(1)}, f32[512,2048]{1,0:T(8,128)}, u32[]{:S(2)}) copy-start(f32[512,2048]{1,0:T(8,128)} %get-tuple-element.132) | copy-start | bytes 12582916 | tf_op jit(solution)/shard_map/while
  96.6 3.4 %copy-start.1 = (f32[512,2048]{1,0:T(8,128)S(1)}, f32[512,2048]{1,0:T(8,128)}, u32[]{:S(2)}) copy-start(f32[512,2048]{1,0:T(8,128)} %get-tuple-element.132) | copy-start | bytes 12582916 | tf_op jit(solution)/shard_map/while
  105.3 12.0 %all-to-all-start.1 = ((f32[32,8,8]{2,1,0:T(8,128)}), f32[32,8,8]{2,1,0:T(8,128)S(1)}, u32[]{:S(2)}, u32[]{:S(2)}) async-start(f32[32,8,8]{2,1,0:T(8,128)} %reshape_reshape.10), calls=%async_computation.1 | async-start | bytes 262144 | tf_op jit(solution)/shard_map/all_to_all | solution.py:72
  128.5 6.6 %copy-start.5 = (bf16[8,32]{1,0:T(8,128)(2,1)S(1)}, bf16[8,32]{1,0:T(8,128)(2,1)}, u32[]{:S(2)}) copy-start(bf16[8,32]{1,0:T(8,128)(2,1)} %param.15) | copy-start | bytes 1540
  128.5 38.1 %copy-start.3 = (bf16[8,8,576]{2,0,1:T(8,128)(2,1)S(1)}, bf16[8,8,576]{2,0,1:T(8,128)(2,1)}, u32[]{:S(2)}) copy-start(bf16[8,8,576]{2,0,1:T(8,128)(2,1)} %pad_maximum_fusion) | copy-start | bytes 221188
  128.5 38.2 %copy-start.7 = (bf16[32]{0:T(256)(128)(2,1)S(1)}, bf16[32]{0:T(256)(128)(2,1)}, u32[]{:S(2)}) copy-start(bf16[32]{0:T(256)(128)(2,1)} %param.17) | copy-start | bytes 196
  128.5 65.8 %copy-start.6 = (bf16[8,64]{1,0:T(8,128)(2,1)S(1)}, bf16[8,64]{1,0:T(8,128)(2,1)}, u32[]{:S(2)}) copy-start(bf16[8,64]{1,0:T(8,128)(2,1)} %param.16) | copy-start | bytes 3076
  128.5 66.5 %copy-start.8 = (s32[2]{0:T(128)S(1)}, s32[2]{0:T(128)}, u32[]{:S(2)}) copy-start(s32[2]{0:T(128)} %param.14) | copy-start | bytes 28
  128.5 66.6 %copy-start.4 = (bf16[2,256,576]{1,2,0:T(8,128)(2,1)S(1)}, bf16[2,256,576]{1,2,0:T(8,128)(2,1)}, u32[]{:S(2)}) copy-start(bf16[2,256,576]{1,2,0:T(8,128)(2,1)} %param.13) | copy-start | bytes 1769476
  128.5 67.7 %all-to-all-start = ((f32[32,8,8,512]{3,2,1,0:T(8,128)}), f32[32,8,8,512]{3,2,1,0:T(8,128)}, u32[]{:S(2)}, u32[]{:S(2)}) async-start(f32[32,8,8,512]{3,2,1,0:T(8,128)} %bitcast.71), calls=%async_computation | async-start | bytes 8388608 | tf_op jit(solution)/shard_map/all_to_all | solution.py:65
  135.1 64.0 %copy-start.2 = (bf16[8,512,128]{2,1,0:T(8,128)(2,1)S(1)}, bf16[8,512,128]{2,1,0:T(8,128)(2,1)}, u32[]{:S(2)}) copy-start(bf16[8,512,128]{2,1,0:T(8,128)(2,1)} %param.19) | copy-start | bytes 3145732
Sparse Core Ops, SparseCore 0:
  10.5 63.7 all-gather.2
where the time goes:
time: 207 us
  blocking collectives  70.1 us (34%)
  waiting for transfers between devices  69.6 us (34%)
  matrix products  20.8 us (10%)
  between operations  13.6 us (7%)
  starting transfers between devices  12.4 us (6%)
  local copies, waits for them, and re-layouts  10.3 us (5%)
  other arithmetic  9.94 us (5%)
    all_gather x1, waiting for transfers between devices, per_device(): every = lax.all_gather(mine, 'seq', axis=0, tiled=True)  63.6 us
    psum x1, blocking collectives, per_device(): squared = lax.psum(jnp.sum(plain * plain, -1), 'head')  31.4 us
    all_gather x1, blocking collectives, per_device(): normed = lax.all_gather(scaled, 'head', axis=1, tiled=True)  27.4 us
    all_to_all x1, blocking collectives, per_device(): lax.all_to_all(mass.reshape(width_seq, local_rows, local_heads), 'seq', s...  11.3 us
    dot_general x2, matrix products, visit(): lax.dot_general(flat, keys, (((1,), (1,)), ((), ())), preferred_element_t...  11.1 us
    dot_general x2, matrix products, visit(): jnp.dot(expd.astype(jnp.bfloat16), keys[:, :latent], preferred_element_ty...  7.25 us
    all_to_all x1, starting transfers between devices, per_device(): lax.all_to_all(accum.reshape(width_seq, local_rows, local_heads, latent),...  6.56 us
    reduce_sum x2, other arithmetic, visit(): mass = mass * fade + jnp.sum(expd, -1)  6.09 us
  transfers between devices with their start and end apart: 3, of which 2 were waited for; matrix products, arithmetic and copies ran while one was open for 2% of the time, Pallas kernels for 0%

commit v1 on v0

v1 whole, which is shorter than its diff:
```python
import functools

import jax
import jax.numpy as jnp
from jax import lax
from jax.experimental import pallas as pl
from jax.experimental.pallas import tpu as pltpu
from jax.sharding import Mesh
from jax.sharding import PartitionSpec as P

eps = 1e-06
LOG2E = 1.4426950408889634
CHIPS = 16
PLANE = ("y", "x")
F32 = jnp.float32
BF16 = jnp.bfloat16
VMEM = pltpu.VMEM
NT = (((1,), (1,)), ((), ()))


def split3(value):
    high = value.astype(BF16).astype(F32)
    rest = value - high
    middle = rest.astype(BF16).astype(F32)
    return high, middle, (rest - middle).astype(BF16).astype(F32)


def pre_kernel(queries_ref, sent_ref):
    by_head = jnp.swapaxes(queries_ref[...].astype(F32), 0, 1)
    rows = by_head.reshape(64, by_head.shape[2]).astype(BF16)
    for chip in range(CHIPS):
        sent_ref[chip] = rows


def main_kernel(scale, q_ref, ka_ref, kb_ref, wuk_ref, wuv_ref, out_ref):
    latent = wuk_ref.shape[2]
    nope = wuk_ref.shape[1]
    lane = lax.broadcasted_iota(jnp.int32, (128, 128), 1)
    stats = jnp.zeros((128, 128), F32)
    for pair in range(4):
        both = q_ref[:, 16 * pair : 16 * pair + 16, :].astype(F32).reshape(CHIPS, 2, 8, -1)
        fulls = []
        for j in range(2):
            one = both[:, j].reshape(128, -1).astype(BF16)
            absorbed = jnp.dot(
                one[:, :nope], wuk_ref[2 * pair + j], preferred_element_type=F32
            ).astype(BF16)
            fulls.append(jnp.concatenate([absorbed, one[:, nope:]], -1))
        full = jnp.concatenate(fulls, 0)
        sa = lax.dot_general(full, ka_ref[...], NT, preferred_element_type=F32)
        sb = lax.dot_general(full, kb_ref[...], NT, preferred_element_type=F32)
        peak = jnp.maximum(jnp.max(sa, -1, keepdims=True), jnp.max(sb, -1, keepdims=True))
        pa = jnp.exp2((sa - peak) * (scale * LOG2E))
        pb = jnp.exp2((sb - peak) * (scale * LOG2E))
        mass = jnp.sum(pa, -1, keepdims=True) + jnp.sum(pb, -1, keepdims=True)
        acc = jnp.dot(pa.astype(BF16), ka_ref[:, :latent], preferred_element_type=F32)
        acc = acc + jnp.dot(pb.astype(BF16), kb_ref[:, :latent], preferred_element_type=F32)
        attn = (acc / mass).astype(BF16)
        values = []
        for j in range(2):
            head = 2 * pair + j
            here = slice(128 * j, 128 * j + 128)
            values.append(
                jnp.dot(attn[here], wuv_ref[head], preferred_element_type=F32).reshape(
                    CHIPS, 8, 128
                )
            )
            for k, piece in enumerate(split3(peak[here]) + split3(mass[here])):
                stats = jnp.where(lane == 8 * k + head, piece, stats)
        out_ref[:, 16 * pair : 16 * pair + 16, :] = jnp.concatenate(values, 1).astype(BF16)
    stats = stats.reshape(CHIPS, 8, 128)
    out_ref[:, 64:80, :] = jnp.concatenate([stats, jnp.zeros_like(stats)], 1).astype(BF16)


def local_kernel(
    scale, q_ref, suffix_ref, lengths_ref, rope_ref, new_ref, wuk_ref, wuv_ref, out_ref, stats_ref
):
    nope, latent = wuk_ref.shape[1:]
    q = q_ref[0]
    width = q.shape[1]
    q32 = q.astype(F32)
    parts = []
    for pair in range(4):
        two = q[16 * pair : 16 * pair + 16, :nope]
        first = jnp.dot(two, wuk_ref[2 * pair], preferred_element_type=F32)
        second = jnp.dot(two, wuk_ref[2 * pair + 1], preferred_element_type=F32)
        parts += [first[:8], second[8:]]
    absorbed = jnp.concatenate(parts, 0)
    full = jnp.concatenate([absorbed, q32[:, nope:]], -1).astype(BF16)

    pieces = new_ref[...].astype(F32)
    new = jnp.concatenate(
        [
            pieces[4 * g] + pieces[4 * g + 1] + pieces[4 * g + 2] + pieces[4 * g + 3]
            for g in range(4)
        ],
        -1,
    )
    plain, gain = new[:8], new[8:9]
    square = jnp.sum(plain * plain, -1, keepdims=True) / latent
    normed = plain * lax.rsqrt(square + eps) * gain
    fresh = jnp.concatenate([normed, rope_ref[...].astype(F32)], -1)
    fresh = jnp.concatenate([fresh, jnp.zeros((120, fresh.shape[1]), F32)], 0).astype(BF16)

    gen = suffix_ref.shape[1]
    row = lax.broadcasted_iota(jnp.int32, (64, gen), 0) % 8
    col = lax.broadcasted_iota(jnp.int32, (64, gen), 1)
    scores, keys = [], []
    for sample in range(2):
        block = suffix_ref[sample]
        raw = lax.dot_general(full, block, NT, preferred_element_type=F32)
        live = (row // 4 == sample) & (col < lengths_ref[sample])
        scores.append(jnp.where(live, raw, -jnp.inf))
        keys.append(block[:, :latent])
    raw = lax.dot_general(full, fresh, NT, preferred_element_type=F32)
    row, col = row[:, :128], col[:, :128]
    live = (col < 8) & (col // 4 == row // 4) & (col <= row)
    scores.append(jnp.where(live, raw, -jnp.inf))
    keys.append(fresh[:, :latent])
    peak = functools.reduce(jnp.maximum, [jnp.max(s, -1, keepdims=True) for s in scores])
    mass, acc = 0.0, 0.0
    for s, v in zip(scores, keys):
        p = jnp.exp2((s - peak) * (scale * LOG2E))
        mass = mass + jnp.sum(p, -1, keepdims=True)
        acc = acc + jnp.dot(p.astype(BF16), v, preferred_element_type=F32)
    attn = (acc / mass).astype(BF16)
    lane = lax.broadcasted_iota(jnp.int32, (8, 128), 1)
    stats = jnp.zeros((8, 128), F32)
    for pair in range(4):
        two = attn[16 * pair : 16 * pair + 16]
        first = jnp.dot(two, wuv_ref[2 * pair], preferred_element_type=F32)
        second = jnp.dot(two, wuv_ref[2 * pair + 1], preferred_element_type=F32)
        out_ref[16 * pair : 16 * pair + 8, :] = first[:8]
        out_ref[16 * pair + 8 : 16 * pair + 16, :] = second[8:]
    for head in range(8):
        here = slice(8 * head, 8 * head + 8)
        stats = jnp.where(lane == head, peak[here], stats)
        stats = jnp.where(lane == 8 + head, mass[here], stats)
    stats_ref[...] = stats


def combine_kernel(scale, got_ref, own_ref, own_stats_ref, out_ref):
    raw = got_ref[:, 64:80, :].astype(F32)[:, :8, :].reshape(128, 128)

    def lanes(k):
        return raw if k == 0 else pltpu.roll(raw, 128 - 8 * k, 1)

    peaks = (lanes(0) + lanes(1) + lanes(2)).reshape(CHIPS, 8, 128)
    masses = (lanes(3) + lanes(4) + lanes(5)).reshape(CHIPS, 8, 128)
    own_peak = own_stats_ref[...]
    own_mass = pltpu.roll(own_peak, 128 - 8, 1)
    peak = jnp.maximum(jnp.max(peaks, 0), own_peak)
    weights = jnp.exp2((peaks - peak[None]) * (scale * LOG2E)) * masses
    own_weight = jnp.exp2((own_peak - peak) * (scale * LOG2E)) * own_mass
    inverse = 1.0 / (jnp.sum(weights, 0) + own_weight)
    for pair in range(4):
        got = got_ref[:, 16 * pair : 16 * pair + 16, :].astype(F32)
        for j in range(2):
            head = 2 * pair + j
            total = own_weight[:, head : head + 1] * own_ref[8 * head : 8 * head + 8, :]
            for chip in range(CHIPS):
                total = total + weights[chip, :, head : head + 1] * got[chip, 8 * j : 8 * j + 8, :]
            total = total * inverse[:, head : head + 1]
            out_ref[:, 128 * head : 128 * head + 128] = total.astype(BF16)


def call(kernel, outs, n_in, smem=()):
    return pl.pallas_call(
        kernel,
        out_shape=outs,
        in_specs=[
            pl.BlockSpec(memory_space=pltpu.SMEM if i in smem else VMEM) for i in range(n_in)
        ],
        out_specs=jax.tree.map(lambda _: pl.BlockSpec(memory_space=VMEM), outs),
        compiler_params=pltpu.CompilerParams(vmem_limit_bytes=48 * 1024 * 1024),
    )


def per_device(
    queries, prompt_cache, suffix_cache, gen_lengths, new_latent, new_rope, latent_gain, w_uk, w_uv
):
    width = queries.shape[2]
    scale = float(width) ** (-0.5)
    other = lax.ppermute(prompt_cache, "core", [(0, 1), (1, 0)])
    sent = call(pre_kernel, jax.ShapeDtypeStruct((CHIPS, 64, width), BF16), 1)(queries)
    gathered = lax.all_to_all(sent, PLANE, 0, 0, tiled=True)

    place = lax.axis_index("z") % 4
    mine = jnp.concatenate([new_latent, latent_gain[None]], 0)
    mine = jnp.tile(jnp.pad(mine, ((0, 7), (0, 0))), (1, 4))
    mine = jnp.where(jnp.arange(128)[None] // 32 == place, mine, 0)
    news = lax.all_to_all(jnp.broadcast_to(mine[None], (16, 16, 128)), "z", 0, 0, tiled=True)

    parts = call(
        functools.partial(main_kernel, scale), jax.ShapeDtypeStruct((CHIPS, 80, 128), BF16), 5
    )(gathered, prompt_cache, other, w_uk, w_uv)
    got = lax.all_to_all(parts, PLANE, 0, 0, tiled=True)
    own, own_stats = call(
        functools.partial(local_kernel, scale),
        (jax.ShapeDtypeStruct((64, 128), F32), jax.ShapeDtypeStruct((8, 128), F32)),
        7,
        smem=(2,),
    )(sent, suffix_cache, gen_lengths, new_rope, news, w_uk, w_uv)
    return call(
        functools.partial(combine_kernel, scale), jax.ShapeDtypeStruct((8, 1024), BF16), 3
    )(got, own, own_stats)


def solution(mesh):
    fine = Mesh(mesh.devices.reshape(4, 4, 2, 16), ("y", "x", "core", "z"))
    seq = ("y", "x", "core")
    return jax.shard_map(
        per_device,
        mesh=fine,
        in_specs=(
            P(seq, "z", None),
            P(seq, None),
            P(seq, None, None),
            P(seq),
            P(seq, "z"),
            P(seq, None),
            P("z"),
            P("z", None, None),
            P("z", None, None),
        ),
        out_specs=P(seq, "z"),
        check_vma=False,
    )
```

time: 207 us -> 66.8 us (0.32)
  the two profiles are of different devices: /device:TPU:6 before, /device:TPU:32 now
where the time goes in v1:
time: 66.8 us; the launch traced here: 66.1 us
  starting transfers between devices  27.8 us (42%)
  waiting for transfers between devices  16.4 us (25%)
  Pallas kernels  12.8 us (19%)
  local copies, waits for them, and re-layouts  8.92 us (13%)
    all_to_all x1, starting transfers between devices, per_device(): lax.all_to_all(jnp.broadcast_to(mine[None], (16, 16, 128)), 'z', 0, 0, ti...  15.2 us
    all_to_all x1, waiting for transfers between devices, per_device(): gathered = lax.all_to_all(sent, PLANE, 0, 0, tiled=True)  12 us
    pallas_call x1, Pallas kernels, per_device(): call(functools.partial(main_kernel, scale), jax.ShapeDtypeStruct((CHIPS,...  8.94 us
    all_to_all x1, starting transfers between devices, per_device(): gathered = lax.all_to_all(sent, PLANE, 0, 0, tiled=True)  7.03 us
    unnamed x22, local copies, waits for them, and re-layouts  6.51 us
    all_to_all x1, waiting for transfers between devices, per_device(): got = lax.all_to_all(parts, PLANE, 0, 0, tiled=True)  4.35 us
    all_to_all x1, starting transfers between devices, per_device(): got = lax.all_to_all(parts, PLANE, 0, 0, tiled=True)  3.69 us
    pallas_call x1, Pallas kernels, per_device(): call(functools.partial(local_kernel, scale), (jax.ShapeDtypeStruct((64, 1...  2.02 us
  transfers between devices with their start and end apart: 4, of which 2 were waited for; matrix products, arithmetic and copies ran while one was open for 7% of the time, Pallas kernels for 18%

profile of v1, /device:TPU:32, one launch (start us, length us, event | category | flops | bytes accessed | tf_op | source)
XLA Modules:
  0.0 66.1 jit_solution(14480098953401763014)
XLA Ops:
  0.0 1.9 %collective-permute-start = (bf16[1024,576]{0,1:T(8,128)(2,1)}, bf16[1024,576]{0,1:T(8,128)(2,1)}, u32[]{:S(2)}, u32[]{:S(2)}) collective-permute-start(bf16[1024,576]{0,1:T(8,128)(2,1)} %param.10), channel_id=1, source_target_pairs={{0,16},{16,0},{1,17},{17,1},{2,18},{18,2},{3,19},{19,3},{4,20},{20... | collective-permute-start | bytes 3538952 | tf_op jit(solution)/shard_map/ppermute | solution.py:184
  1.9 0.0 copy-start.4
  1.9 0.7 %copy-done.4 = bf16[8,8,192]{2,1,0:T(8,128)(2,1)S(1)} copy-done((bf16[8,8,192]{2,1,0:T(8,128)(2,1)S(1)}, bf16[8,8,192]{2,1,0:T(8,128)(2,1)}, u32[]{:S(2)}) %copy-start.4) | copy-done | bytes 24600
  2.7 0.0 copy-start.8
  2.7 0.0 copy-start.9
  2.7 0.0 copy-start.7
  2.7 0.9 %shard_map.91.q_ref = bf16[16,64,192]{2,1,0:T(8,128)(2,1)} custom-call(bf16[8,8,192]{2,1,0:T(8,128)(2,1)S(1)} %copy-done.4), custom_call_target="tpu_custom_call" | custom-call | tf_op jit(solution)/shard_map/pallas_call | solution.py:185
  3.5 7.0 %all-to-all-start = ((bf16[16,64,192]{2,1,0:T(8,128)(2,1)}), bf16[16,64,192]{2,1,0:T(8,128)(2,1)S(1)}, u32[]{:S(2)}, u32[]{:S(2)}) async-start(bf16[16,64,192]{2,1,0:T(8,128)(2,1)} %shard_map.91.q_ref), calls=%async_computation | async-start | bytes 1048576 | tf_op jit(solution)/shard_map/all_to_all | solution.py:186
  10.6 0.0 copy-done.8
  10.6 0.0 copy-done.9
  10.7 0.1 tile.10
  10.8 12.0 %all-to-all-done.q_ref = bf16[16,64,192]{2,1,0:T(8,128)(2,1)S(1)} async-done(((bf16[16,64,192]{2,1,0:T(8,128)(2,1)}), bf16[16,64,192]{2,1,0:T(8,128)(2,1)S(1)}, u32[]{:S(2)}, u32[]{:S(2)}) %all-to-all-start) | async-done | bytes 393248 | tf_op jit(solution)/shard_map/all_to_all | solution.py:186
  22.8 0.6 broadcast_in_dim.25
  23.4 15.2 %all-to-all-start.2 = ((bf16[16,16,128]{2,1,0:T(8,128)(2,1)}), bf16[16,16,128]{2,1,0:T(8,128)(2,1)S(1)}, u32[]{:S(2)}, u32[]{:S(2)}) async-start(bf16[16,16,128]{2,1,0:T(8,128)(2,1)} %broadcast_in_dim.25), calls=%async_computation.2 | async-start | bytes 131072 | tf_op jit(solution)/shard_map/all_to_all | solution.py:192
  38.6 0.0 copy-done.7
  38.6 0.7 %copy.13.ka_ref = bf16[1024,576]{1,0:T(8,128)(2,1)S(1)} copy(bf16[1024,576]{0,1:T(8,128)(2,1)S(1)} %copy-done.7) | data formatting | bytes 2359296 | tf_op args[1]
  39.4 0.0 collective-permute-done
  39.4 1.7 %copy.14.kb_ref = bf16[1024,576]{1,0:T(8,128)(2,1)S(1)} copy(bf16[1024,576]{0,1:T(8,128)(2,1)} %collective-permute-done) | data formatting | bytes 2359296 | tf_op jit(solution)/shard_map/ppermute | solution.py:184
  41.1 0.0 copy-start
  41.1 1.2 %copy-done = bf16[8,128,512]{2,1,0:T(8,128)(2,1)S(1)} copy-done((bf16[8,128,512]{2,1,0:T(8,128)(2,1)S(1)}, bf16[8,128,512]{2,1,0:T(8,128)(2,1)}, u32[]{:S(2)}) %copy-start) | copy-done | bytes 1048600
  42.3 0.0 copy-start.2
  42.3 1.2 %copy-done.2 = bf16[8,512,128]{2,1,0:T(8,128)(2,1)S(1)} copy-done((bf16[8,512,128]{2,1,0:T(8,128)(2,1)S(1)}, bf16[8,512,128]{2,1,0:T(8,128)(2,1)}, u32[]{:S(2)}) %copy-start.2) | copy-done | bytes 1048600
  43.5 8.9 %shard_map.92 = bf16[16,80,128]{2,1,0:T(8,128)(2,1)} custom-call(bf16[16,64,192]{2,1,0:T(8,128)(2,1)S(1)} %all-to-all-done.q_ref, bf16[1024,576]{1,0:T(8,128)(2,1)S(1)} %copy.13.ka_ref, bf16[1024,576]{1,0:T(8,128)(2,1)S(1)} %copy.14.kb_ref, bf16[8,128,512]{2,1,0:T(8,128)(2,1)S(1)} %copy-done, bf16[8,512,128]{2,1,0:T(8,128)(2,1)S(1)} %copy-done.2), custom_call_target="tpu_custom_call" | custom-call | tf_op jit(solution)/shard_map/pallas_call | solution.py:194
  52.5 0.0 copy-start.1
  52.5 0.0 copy-start.5
  52.5 0.0 copy-start.6
  52.5 0.0 all-to-all-done.2.new_ref
  52.5 3.7 %all-to-all-start.1 = ((bf16[16,80,128]{2,1,0:T(8,128)(2,1)}), bf16[16,80,128]{2,1,0:T(8,128)(2,1)S(1)}, u32[]{:S(2)}, u32[]{:S(2)}) async-start(bf16[16,80,128]{2,1,0:T(8,128)(2,1)} %shard_map.92), calls=%async_computation.1 | async-start | bytes 655360 | tf_op jit(solution)/shard_map/all_to_all | solution.py:197
  56.2 1.4 %copy.15.suffix_ref = bf16[2,256,576]{2,1,0:T(8,128)(2,1)S(1)} copy(bf16[2,256,576]{1,2,0:T(8,128)(2,1)} %param.11) | data formatting | bytes 1179648 | tf_op args[2]
  57.5 0.0 copy-done.1
  57.5 0.0 copy-done.5
  57.5 0.0 copy-done.6
  57.5 0.0 copy-start.3
  57.6 1.2 %copy-done.3 = bf16[8,512,128]{2,1,0:T(8,128)(2,1)S(1)} copy-done((bf16[8,512,128]{2,1,0:T(8,128)(2,1)S(1)}, bf16[8,512,128]{2,1,0:T(8,128)(2,1)}, u32[]{:S(2)}) %copy-start.3) | copy-done | bytes 1048600
  58.8 2.0 %shard_map.93 = (f32[64,128]{1,0:T(8,128)S(1)}, f32[8,128]{1,0:T(8,128)S(1)}) custom-call(bf16[16,64,192]{2,1,0:T(8,128)(2,1)} %shard_map.91.q_ref, bf16[2,256,576]{2,1,0:T(8,128)(2,1)S(1)} %copy.15.suffix_ref, s32[2]{0:T(128)S(1)} %copy-done.6, bf16[8,64]{1,0:T(8,128)(2,1)S(1)} %copy-done.5, bf16[16,16,128]{2,1,0:T(8,128)(2,1)S(1)} %all-to-all-done.2.new_ref, ...), custom_call_target="tpu_custom_call" | custom-call | tf_op jit(solution)/shard_map/pallas_call | solution.py:198
  60.8 4.4 %all-to-all-done.1.got_ref = bf16[16,80,128]{2,1,0:T(8,128)(2,1)S(1)} async-done(((bf16[16,80,128]{2,1,0:T(8,128)(2,1)}), bf16[16,80,128]{2,1,0:T(8,128)(2,1)S(1)}, u32[]{:S(2)}, u32[]{:S(2)}) %all-to-all-start.1) | async-done | bytes 327712 | tf_op jit(solution)/shard_map/all_to_all | solution.py:197
  65.2 1.0 %shard_map.94 = bf16[8,1024]{1,0:T(8,128)(2,1)} custom-call(bf16[16,80,128]{2,1,0:T(8,128)(2,1)S(1)} %all-to-all-done.1.got_ref, f32[64,128]{1,0:T(8,128)S(1)} %get-tuple-element.7.own_ref, f32[8,128]{1,0:T(8,128)S(1)} %get-tuple-element.8.own_stats_ref), custom_call_target="tpu_custom_call" | custom-call | tf_op jit(solution)/shard_map/pallas_call | solution.py:204
  (4 shorter events, 0.0 us)
Async XLA Ops:
  0.0 39.4 %collective-permute-start = (bf16[1024,576]{0,1:T(8,128)(2,1)}, bf16[1024,576]{0,1:T(8,128)(2,1)}, u32[]{:S(2)}, u32[]{:S(2)}) collective-permute-start(bf16[1024,576]{0,1:T(8,128)(2,1)} %param.10), channel_id=1, source_target_pairs={{0,16},{16,0},{1,17},{17,1},{2,18},{18,2},{3,19},{19,3},{4,20},{20... | collective-permute-start | bytes 3538952 | tf_op jit(solution)/shard_map/ppermute | solution.py:184
  1.9 0.8 %copy-start.4 = (bf16[8,8,192]{2,1,0:T(8,128)(2,1)S(1)}, bf16[8,8,192]{2,1,0:T(8,128)(2,1)}, u32[]{:S(2)}) copy-start(bf16[8,8,192]{2,1,0:T(8,128)(2,1)} %queries_ref.1) | copy-start | bytes 73732
  2.7 7.9 %copy-start.8 = (bf16[8,32]{1,0:T(8,128)(2,1)S(1)}, bf16[8,32]{1,0:T(8,128)(2,1)}, u32[]{:S(2)}) copy-start(bf16[8,32]{1,0:T(8,128)(2,1)} %param.13) | copy-start | bytes 1540
  2.7 7.9 %copy-start.9 = (bf16[32]{0:T(256)(128)(2,1)S(1)}, bf16[32]{0:T(256)(128)(2,1)}, u32[]{:S(2)}) copy-start(bf16[32]{0:T(256)(128)(2,1)} %param.15) | copy-start | bytes 196
  2.7 35.9 %copy-start.7 = (bf16[1024,576]{0,1:T(8,128)(2,1)S(1)}, bf16[1024,576]{0,1:T(8,128)(2,1)}, u32[]{:S(2)}) copy-start(bf16[1024,576]{0,1:T(8,128)(2,1)} %param.10) | copy-start | bytes 3538948
  3.5 19.2 %all-to-all-start = ((bf16[16,64,192]{2,1,0:T(8,128)(2,1)}), bf16[16,64,192]{2,1,0:T(8,128)(2,1)S(1)}, u32[]{:S(2)}, u32[]{:S(2)}) async-start(bf16[16,64,192]{2,1,0:T(8,128)(2,1)} %shard_map.91.q_ref), calls=%async_computation | async-start | bytes 1048576 | tf_op jit(solution)/shard_map/all_to_all | solution.py:186
  23.4 29.0 %all-to-all-start.2 = ((bf16[16,16,128]{2,1,0:T(8,128)(2,1)}), bf16[16,16,128]{2,1,0:T(8,128)(2,1)S(1)}, u32[]{:S(2)}, u32[]{:S(2)}) async-start(bf16[16,16,128]{2,1,0:T(8,128)(2,1)} %broadcast_in_dim.25), calls=%async_computation.2 | async-start | bytes 131072 | tf_op jit(solution)/shard_map/all_to_all | solution.py:192
  41.1 1.2 %copy-start = (bf16[8,128,512]{2,1,0:T(8,128)(2,1)S(1)}, bf16[8,128,512]{2,1,0:T(8,128)(2,1)}, u32[]{:S(2)}) copy-start(bf16[8,128,512]{2,1,0:T(8,128)(2,1)} %wuk_ref.3) | copy-start | bytes 3145732
  42.3 1.2 %copy-start.2 = (bf16[8,512,128]{2,1,0:T(8,128)(2,1)S(1)}, bf16[8,512,128]{2,1,0:T(8,128)(2,1)}, u32[]{:S(2)}) copy-start(bf16[8,512,128]{2,1,0:T(8,128)(2,1)} %wuv_ref.3) | copy-start | bytes 3145732
  52.5 5.1 %copy-start.1 = (bf16[8,128,512]{2,1,0:T(8,128)(2,1)S(1)}, bf16[8,128,512]{2,1,0:T(8,128)(2,1)}, u32[]{:S(2)}) copy-start(bf16[8,128,512]{2,1,0:T(8,128)(2,1)} %wuk_ref.3) | copy-start | bytes 3145732
  52.5 5.1 %copy-start.5 = (bf16[8,64]{1,0:T(8,128)(2,1)S(1)}, bf16[8,64]{1,0:T(8,128)(2,1)}, u32[]{:S(2)}) copy-start(bf16[8,64]{1,0:T(8,128)(2,1)} %rope_ref.1) | copy-start | bytes 3076
  52.5 5.1 %copy-start.6 = (s32[2]{0:T(128)S(1)}, s32[2]{0:T(128)}, u32[]{:S(2)}) copy-start(s32[2]{0:T(128)} %lengths_ref.1) | copy-start | bytes 28
  52.5 12.7 %all-to-all-start.1 = ((bf16[16,80,128]{2,1,0:T(8,128)(2,1)}), bf16[16,80,128]{2,1,0:T(8,128)(2,1)S(1)}, u32[]{:S(2)}, u32[]{:S(2)}) async-start(bf16[16,80,128]{2,1,0:T(8,128)(2,1)} %shard_map.92), calls=%async_computation.1 | async-start | bytes 655360 | tf_op jit(solution)/shard_map/all_to_all | solution.py:197
  57.5 1.2 %copy-start.3 = (bf16[8,512,128]{2,1,0:T(8,128)(2,1)S(1)}, bf16[8,512,128]{2,1,0:T(8,128)(2,1)}, u32[]{:S(2)}) copy-start(bf16[8,512,128]{2,1,0:T(8,128)(2,1)} %wuv_ref.3) | copy-start | bytes 3145732

commit v2 on v1

v2 whole, which is shorter than its diff:
```python
import functools

import jax
import jax.numpy as jnp
from jax import lax
from jax.experimental import pallas as pl
from jax.experimental.pallas import tpu as pltpu
from jax.sharding import Mesh
from jax.sharding import PartitionSpec as P

eps = 1e-06
LOG2E = 1.4426950408889634
CHIPS = 16
PLANE = ("y", "x")
F32 = jnp.float32
BF16 = jnp.bfloat16
VMEM = pltpu.VMEM
NT = (((1,), (1,)), ((), ()))


def split3(value):
    high = value.astype(BF16).astype(F32)
    rest = value - high
    middle = rest.astype(BF16).astype(F32)
    return high, middle, (rest - middle).astype(BF16).astype(F32)


def queries_kernel(queries_ref, sent_ref):
    by_head = jnp.swapaxes(queries_ref[...].astype(F32), 0, 1)
    rows = by_head.reshape(64, by_head.shape[2]).astype(BF16)
    for chip in range(CHIPS):
        sent_ref[chip] = rows


def own_kernel(q_ref, latent_ref, gain_ref, wuk_ref, mine_ref, full_ref):
    latents = latent_ref[...].astype(F32)
    gain = jnp.concatenate([gain_ref[...].astype(F32), jnp.zeros((3, 32), F32)], 0)
    mine = [latents[:4], latents[4:], gain, jnp.zeros((4, 32), F32)]
    mine = jnp.concatenate(mine, 1).astype(BF16)
    for device in range(16):
        mine_ref[device] = mine
    nope = wuk_ref.shape[1]
    q = q_ref[0]
    parts = []
    for pair in range(4):
        two = q[16 * pair : 16 * pair + 16, :nope]
        first = jnp.dot(two, wuk_ref[2 * pair], preferred_element_type=F32)
        second = jnp.dot(two, wuk_ref[2 * pair + 1], preferred_element_type=F32)
        parts += [first[:8], second[8:]]
    absorbed = jnp.concatenate(parts, 0)
    full_ref[...] = jnp.concatenate([absorbed, q[:, nope:].astype(F32)], -1).astype(BF16)


def main_kernel(
    scale,
    q_hbm,
    ka_hbm,
    kb_hbm,
    wuk_hbm,
    wuv_hbm,
    out_ref,
    q_ref,
    ka_ref,
    kb_ref,
    wuk_ref,
    wuv_ref,
    sems,
):
    copies = [
        pltpu.make_async_copy(source, target, sems.at[i])
        for i, (source, target) in enumerate(
            [
                (q_hbm, q_ref),
                (wuk_hbm.at[:2], wuk_ref.at[:2]),
                (ka_hbm, ka_ref),
                (wuk_hbm.at[2:], wuk_ref.at[2:]),
                (kb_hbm, kb_ref),
                (wuv_hbm, wuv_ref),
            ]
        )
    ]
    for copy in copies:
        copy.start()
    nope, latent = wuk_ref.shape[1:]

    def absorb(pair):
        both = q_ref[:, 16 * pair : 16 * pair + 16, :].astype(F32).reshape(CHIPS, 2, 8, -1)
        fulls = []
        for j in range(2):
            one = both[:, j].reshape(128, -1).astype(BF16)
            absorbed = jnp.dot(
                one[:, :nope], wuk_ref[2 * pair + j], preferred_element_type=F32
            ).astype(BF16)
            fulls.append(jnp.concatenate([absorbed, one[:, nope:]], -1))
        return fulls

    copies[0].wait()
    copies[1].wait()
    fulls = absorb(0)
    copies[2].wait()
    copies[3].wait()
    for pair in range(1, 4):
        fulls += absorb(pair)
    full = jnp.concatenate(fulls, 0)

    half = ka_ref.shape[1] // 2
    blocks = [(keys, i * half) for keys in (ka_ref, kb_ref) for i in range(2)]

    def score(keys, at):
        return jnp.dot(full, keys[:, at : at + half], preferred_element_type=F32)

    scores = score(*blocks[0])
    peak = None
    for i, (keys, at) in enumerate(blocks):
        if i == 0:
            copies[4].wait()
            copies[5].wait()
        later = score(*blocks[i + 1]) if i < 3 else None
        top = jnp.max(scores, -1, keepdims=True)
        top = top if peak is None else jnp.maximum(peak, top)
        expd = jnp.exp2((scores - top) * (scale * LOG2E))
        part = lax.dot_general(
            expd.astype(BF16), keys[:latent, at : at + half], NT, preferred_element_type=F32
        )
        if peak is None:
            mass, acc = jnp.sum(expd, -1, keepdims=True), part
        else:
            fade = jnp.exp2((peak - top) * (scale * LOG2E))
            mass = mass * fade + jnp.sum(expd, -1, keepdims=True)
            acc = acc * fade + part
        peak, scores = top, later

    attn = (acc / mass).astype(BF16)
    lane = lax.broadcasted_iota(jnp.int32, (128, 128), 1)
    stats = jnp.zeros((128, 128), F32)
    for pair in range(4):
        values = []
        for j in range(2):
            head = 2 * pair + j
            here = slice(128 * head, 128 * head + 128)
            values.append(
                jnp.dot(attn[here], wuv_ref[head], preferred_element_type=F32).reshape(
                    CHIPS, 8, 128
                )
            )
            for k, piece in enumerate(split3(peak[here]) + split3(mass[here])):
                stats = jnp.where(lane == 8 * k + head, piece, stats)
        out_ref[:, 16 * pair : 16 * pair + 16, :] = jnp.concatenate(values, 1).astype(BF16)
    stats = stats.reshape(CHIPS, 8, 128)
    out_ref[:, 64:80, :] = jnp.concatenate([stats, jnp.zeros_like(stats)], 1).astype(BF16)


def local_kernel(
    scale, full_ref, suffix_ref, lengths_ref, rope_ref, new_ref, wuv_ref, out_ref, stats_ref
):
    latent = wuv_ref.shape[1]
    full = full_ref[...]
    pieces = new_ref[...].astype(F32)
    lane = lax.broadcasted_iota(jnp.int32, (4, 128), 1) // 32
    parts = []
    for k in range(3):
        groups = []
        for g in range(4):
            group = 0.0
            for j in range(4):
                only = jnp.where(lane == k, pieces[4 * g + j], 0.0)
                shift = (32 * (j - k)) % 128
                group = group + (pltpu.roll(only, shift, 1) if shift else only)
            groups.append(group)
        parts.append(jnp.concatenate(groups, -1))
    new = jnp.concatenate(parts, 0)
    plain, gain = new[:8], new[8:9]
    square = jnp.sum(plain * plain, -1, keepdims=True) / latent
    normed = plain * lax.rsqrt(square + eps) * gain
    fresh = jnp.concatenate([normed, rope_ref[...].astype(F32)], -1)
    fresh = jnp.concatenate([fresh, jnp.zeros((120, fresh.shape[1]), F32)], 0).astype(BF16)

    gen = suffix_ref.shape[2]
    row = lax.broadcasted_iota(jnp.int32, (64, gen), 0) % 8
    col = lax.broadcasted_iota(jnp.int32, (64, gen), 1)
    scores, keys = [], []
    for sample in range(2):
        block = suffix_ref[sample]
        raw = jnp.dot(full, block, preferred_element_type=F32)
        live = (row // 4 == sample) & (col < lengths_ref[sample])
        scores.append(jnp.where(live, raw, -jnp.inf))
        keys.append(block[:latent])
    raw = lax.dot_general(full, fresh, NT, preferred_element_type=F32)
    row, col = row[:, :128], col[:, :128]
    live = (col < 8) & (col // 4 == row // 4) & (col <= row)
    scores.append(jnp.where(live, raw, -jnp.inf))
    keys.append(fresh[:, :latent].T)
    peak = functools.reduce(jnp.maximum, [jnp.max(s, -1, keepdims=True) for s in scores])
    mass, acc = 0.0, 0.0
    for s, v in zip(scores, keys):
        p = jnp.exp2((s - peak) * (scale * LOG2E))
        mass = mass + jnp.sum(p, -1, keepdims=True)
        acc = acc + lax.dot_general(p.astype(BF16), v, NT, preferred_element_type=F32)
    attn = (acc / mass).astype(BF16)
    lane = lax.broadcasted_iota(jnp.int32, (8, 128), 1)
    stats = jnp.zeros((8, 128), F32)
    for pair in range(4):
        two = attn[16 * pair : 16 * pair + 16]
        first = jnp.dot(two, wuv_ref[2 * pair], preferred_element_type=F32)
        second = jnp.dot(two, wuv_ref[2 * pair + 1], preferred_element_type=F32)
        out_ref[16 * pair : 16 * pair + 8, :] = first[:8]
        out_ref[16 * pair + 8 : 16 * pair + 16, :] = second[8:]
    for head in range(8):
        here = slice(8 * head, 8 * head + 8)
        stats = jnp.where(lane == head, peak[here], stats)
        stats = jnp.where(lane == 8 + head, mass[here], stats)
    stats_ref[...] = stats


def combine_kernel(scale, got_ref, own_ref, own_stats_ref, out_ref):
    raw = got_ref[:, 64:80, :].astype(F32)[:, :8, :].reshape(128, 128)

    def lanes(k):
        return raw if k == 0 else pltpu.roll(raw, 128 - 8 * k, 1)

    peaks = (lanes(0) + lanes(1) + lanes(2)).reshape(CHIPS, 8, 128)
    masses = (lanes(3) + lanes(4) + lanes(5)).reshape(CHIPS, 8, 128)
    own_peak = own_stats_ref[...]
    own_mass = pltpu.roll(own_peak, 128 - 8, 1)
    peak = jnp.maximum(jnp.max(peaks, 0), own_peak)
    weights = jnp.exp2((peaks - peak[None]) * (scale * LOG2E)) * masses
    own_weight = jnp.exp2((own_peak - peak) * (scale * LOG2E)) * own_mass
    inverse = 1.0 / (jnp.sum(weights, 0) + own_weight)
    for pair in range(4):
        got = got_ref[:, 16 * pair : 16 * pair + 16, :].astype(F32)
        for j in range(2):
            head = 2 * pair + j
            total = own_weight[:, head : head + 1] * own_ref[8 * head : 8 * head + 8, :]
            for chip in range(CHIPS):
                total = total + weights[chip, :, head : head + 1] * got[chip, 8 * j : 8 * j + 8, :]
            total = total * inverse[:, head : head + 1]
            out_ref[:, 128 * head : 128 * head + 128] = total.astype(BF16)


def call(kernel, outs, n_in, smem=(), hbm=(), scratch=(), cost=1, mib=24):
    spaces = [pltpu.SMEM if i in smem else pl.ANY if i in hbm else VMEM for i in range(n_in)]
    return pl.pallas_call(
        kernel,
        out_shape=outs,
        in_specs=[pl.BlockSpec(memory_space=space) for space in spaces],
        out_specs=jax.tree.map(lambda _: pl.BlockSpec(memory_space=VMEM), outs),
        scratch_shapes=scratch,
        compiler_params=pltpu.CompilerParams(vmem_limit_bytes=mib * 1024 * 1024),
        cost_estimate=pl.CostEstimate(
            flops=cost * 10**9, transcendentals=0, bytes_accessed=0
        ),
    )


def per_device(
    queries, prompt_cache, suffix_cache, gen_lengths, new_latent, new_rope, latent_gain, w_uk, w_uv
):
    width = queries.shape[2]
    scale = float(width) ** (-0.5)
    sent = call(queries_kernel, jax.ShapeDtypeStruct((CHIPS, 64, width), BF16), 1)(queries)
    mine, full = call(
        own_kernel,
        (
            jax.ShapeDtypeStruct((16, 4, 128), BF16),
            jax.ShapeDtypeStruct((64, prompt_cache.shape[1]), BF16),
        ),
        4,
        cost=30,
    )(sent, new_latent, latent_gain[None], w_uk)
    gathered = lax.all_to_all(sent, PLANE, 0, 0, tiled=True)
    keys = prompt_cache.T
    other = lax.ppermute(keys, "core", [(0, 1), (1, 0)])
    news = lax.all_to_all(mine, "z", 0, 0, tiled=True)
    parts = call(
        functools.partial(main_kernel, scale),
        jax.ShapeDtypeStruct((CHIPS, 80, 128), BF16),
        5,
        hbm=(0, 1, 2, 3, 4),
        scratch=[
            VMEM(gathered.shape, BF16),
            VMEM(keys.shape, BF16),
            VMEM(keys.shape, BF16),
            VMEM(w_uk.shape, BF16),
            VMEM(w_uv.shape, BF16),
            pltpu.SemaphoreType.DMA((6,)),
        ],
        cost=8,
        mib=59,
    )(gathered, keys, other, w_uk, w_uv)
    got = lax.all_to_all(parts, PLANE, 0, 0, tiled=True)
    own, own_stats = call(
        functools.partial(local_kernel, scale),
        (jax.ShapeDtypeStruct((64, 128), F32), jax.ShapeDtypeStruct((8, 128), F32)),
        6,
        smem=(2,),
    )(full, jnp.swapaxes(suffix_cache, 1, 2), gen_lengths, new_rope, news, w_uv)
    return call(
        functools.partial(combine_kernel, scale), jax.ShapeDtypeStruct((8, 1024), BF16), 3
    )(got, own, own_stats)


def solution(mesh):
    fine = Mesh(mesh.devices.reshape(4, 4, 2, 16), ("y", "x", "core", "z"))
    seq = ("y", "x", "core")
    return jax.shard_map(
        per_device,
        mesh=fine,
        in_specs=(
            P(seq, "z", None),
            P(seq, None),
            P(seq, None, None),
            P(seq),
            P(seq, "z"),
            P(seq, None),
            P("z"),
            P("z", None, None),
            P("z", None, None),
        ),
        out_specs=P(seq, "z"),
        check_vma=False,
    )
```

time: 66.8 us -> 61.1 us (0.915)
  the two profiles are of different devices: /device:TPU:32 before, /device:TPU:2 now
where the time goes in v2:
time: 61.1 us; the launch traced here: 60.6 us
  starting transfers between devices  30.7 us (50%)
  Pallas kernels  14.7 us (24%)
  waiting for transfers between devices  14.2 us (23%)
  local copies, waits for them, and re-layouts  0.89 us (1%)
    all_to_all x1, starting transfers between devices, per_device(): news = lax.all_to_all(mine, 'z', 0, 0, tiled=True)  14.8 us
    pallas_call x1, Pallas kernels, per_device(): call(functools.partial(main_kernel, scale), jax.ShapeDtypeStruct((CHIPS,...  9.65 us
    all_to_all x1, starting transfers between devices, per_device(): gathered = lax.all_to_all(sent, PLANE, 0, 0, tiled=True)  9.27 us
    all_to_all x1, waiting for transfers between devices, per_device(): got = lax.all_to_all(parts, PLANE, 0, 0, tiled=True)  6.35 us
    all_to_all x1, waiting for transfers between devices, per_device(): gathered = lax.all_to_all(sent, PLANE, 0, 0, tiled=True)  5.07 us
    all_to_all x1, starting transfers between devices, per_device(): got = lax.all_to_all(parts, PLANE, 0, 0, tiled=True)  4.79 us
    all_to_all x1, waiting for transfers between devices, per_device(): news = lax.all_to_all(mine, 'z', 0, 0, tiled=True)  2.81 us
    ppermute x1, starting transfers between devices, per_device(): other = lax.ppermute(keys, 'core', [(0, 1), (1, 0)])  1.91 us
  transfers between devices with their start and end apart: 4, of which 3 were waited for; matrix products, arithmetic and copies ran while one was open for 0% of the time, Pallas kernels for 21%

profile of v2, /device:TPU:2, one launch (start us, length us, event | category | flops | bytes accessed | tf_op | source)
XLA Modules:
  0.0 60.6 jit_solution(1929062678459243963)
XLA Ops:
  0.0 0.0 copy-start
  0.0 0.0 copy-start.3
  0.0 0.8 %copy-done.3 = bf16[8,8,192]{2,1,0:T(8,128)(2,1)S(1)} copy-done((bf16[8,8,192]{2,1,0:T(8,128)(2,1)S(1)}, bf16[8,8,192]{2,1,0:T(8,128)(2,1)}, u32[]{:S(2)}) %copy-start.3) | copy-done | bytes 24600
  0.8 0.0 copy-start.4
  0.9 0.0 copy-start.6
  0.9 0.9 %shard_map.91.q_ref = bf16[16,64,192]{2,1,0:T(8,128)(2,1)} custom-call(bf16[8,8,192]{2,1,0:T(8,128)(2,1)S(1)} %copy-done.3), custom_call_target="tpu_custom_call" | custom-call | flops 1000000000 | tf_op jit(solution)/shard_map/pallas_call | solution.py:260
  1.7 9.3 %all-to-all-start = ((bf16[16,64,192]{2,1,0:T(8,128)(2,1)}), bf16[16,64,192]{2,1,0:T(8,128)(2,1)S(1)}, u32[]{:S(2)}, u32[]{:S(2)}) async-start(bf16[16,64,192]{2,1,0:T(8,128)(2,1)} %shard_map.91.q_ref), calls=%async_computation | async-start | bytes 1048576 | tf_op jit(solution)/shard_map/all_to_all | solution.py:270
  11.0 1.9 %collective-permute-start = (bf16[576,1024]{1,0:T(8,128)(2,1)}, bf16[576,1024]{1,0:T(8,128)(2,1)}, u32[]{:S(2)}, u32[]{:S(2)}) collective-permute-start(bf16[576,1024]{1,0:T(8,128)(2,1)} %bitcast.ka_hbm), channel_id=1, source_target_pairs={{0,16},{16,0},{1,17},{17,1},{2,18},{18,2},{3,19},{19,3},{4,20},{20... | collective-permute-start | bytes 3538952 | tf_op jit(solution)/shard_map/ppermute | solution.py:272
  12.9 0.0 copy-done
  12.9 0.0 copy-done.4
  12.9 0.0 copy-done.6
  12.9 1.8 %shard_map.93 = (bf16[16,4,128]{2,1,0:T(4,128)(2,1)}, bf16[64,576]{1,0:T(8,128)(2,1)S(1)}) custom-call(bf16[16,64,192]{2,1,0:T(8,128)(2,1)} %shard_map.91.q_ref, bf16[8,32]{1,0:T(8,128)(2,1)S(1)} %copy-done.4, bf16[1,32]{1,0:T(2,128)(2,1)S(1)} %bitcast.4, bf16[8,128,512]{2,1,0:T(8,128)(2,1)S(1)} %copy-done), custom_call_target="tpu_custom_call" | custom-call | flops 30000001024 | tf_op jit(solution)/shard_map/pallas_call | solution.py:261
  14.7 5.1 %all-to-all-done.q_hbm = bf16[16,64,192]{2,1,0:T(8,128)(2,1)S(1)} async-done(((bf16[16,64,192]{2,1,0:T(8,128)(2,1)}), bf16[16,64,192]{2,1,0:T(8,128)(2,1)S(1)}, u32[]{:S(2)}, u32[]{:S(2)}) %all-to-all-start) | async-done | bytes 393248 | tf_op jit(solution)/shard_map/all_to_all | solution.py:270
  19.8 0.0 copy-start.8
  19.8 14.8 %all-to-all-start.2 = ((bf16[16,4,128]{2,1,0:T(4,128)(2,1)}), bf16[16,4,128]{2,1,0:T(4,128)(2,1)S(1)}, u32[]{:S(2)}, u32[]{:S(2)}) async-start(bf16[16,4,128]{2,1,0:T(4,128)(2,1)} %get-tuple-element.10), calls=%async_computation.2 | async-start | bytes 32768 | tf_op jit(solution)/shard_map/all_to_all | solution.py:273
  34.6 0.0 copy-start.1
  34.6 0.0 copy-start.2
  34.6 0.0 copy-start.5
  34.6 0.0 copy-start.7
  34.6 0.0 collective-permute-done.kb_hbm
  34.6 0.0 copy-done.8
  34.6 9.7 %shard_map.92 = bf16[16,80,128]{2,1,0:T(8,128)(2,1)} custom-call(bf16[16,64,192]{2,1,0:T(8,128)(2,1)} %copy-done.8, bf16[576,1024]{1,0:T(8,128)(2,1)} %bitcast.ka_hbm, bf16[576,1024]{1,0:T(8,128)(2,1)} %collective-permute-done.kb_hbm, bf16[8,128,512]{2,1,0:T(8,128)(2,1)} %wuk_ref.1, bf16[8,512,128]{2,1,0:T(8,128)(2,1)} %wuv_ref.1), custom_call_target="tpu_custom_call" | custom-call | flops 8000000000 | tf_op jit(solution)/shard_map/pallas_call | solution.py:274
  44.3 2.8 %all-to-all-done.2.new_ref = bf16[16,4,128]{2,1,0:T(4,128)(2,1)S(1)} async-done(((bf16[16,4,128]{2,1,0:T(4,128)(2,1)}), bf16[16,4,128]{2,1,0:T(4,128)(2,1)S(1)}, u32[]{:S(2)}, u32[]{:S(2)}) %all-to-all-start.2) | async-done | bytes 16416 | tf_op jit(solution)/shard_map/all_to_all | solution.py:273
  47.1 4.8 %all-to-all-start.1 = ((bf16[16,80,128]{2,1,0:T(8,128)(2,1)}), bf16[16,80,128]{2,1,0:T(8,128)(2,1)S(1)}, u32[]{:S(2)}, u32[]{:S(2)}) async-start(bf16[16,80,128]{2,1,0:T(8,128)(2,1)} %shard_map.92), calls=%async_computation.1 | async-start | bytes 655360 | tf_op jit(solution)/shard_map/all_to_all | solution.py:290
  51.9 0.0 copy-done.1
  51.9 0.0 copy-done.2
  51.9 0.0 copy-done.5
  51.9 0.0 copy-done.7
  51.9 1.4 %shard_map.94 = (f32[64,128]{1,0:T(8,128)S(1)}, f32[8,128]{1,0:T(8,128)S(1)}) custom-call(bf16[64,576]{1,0:T(8,128)(2,1)S(1)} %get-tuple-element.9.full_ref, bf16[2,576,256]{2,1,0:T(8,128)(2,1)S(1)} %bitcast.3, s32[2]{0:T(128)S(1)} %copy-done.7, bf16[8,64]{1,0:T(8,128)(2,1)S(1)} %copy-done.5, bf16[16,4,128]{2,1,0:T(4,128)(2,1)S(1)} %all-to-all-done.2.new_ref, ...), custom_call_target="tpu_custom_call" | custom-call | flops 1000000000 | tf_op jit(solution)/shard_map/pallas_call | solution.py:291
  53.3 6.3 %all-to-all-done.1.got_ref = bf16[16,80,128]{2,1,0:T(8,128)(2,1)S(1)} async-done(((bf16[16,80,128]{2,1,0:T(8,128)(2,1)}), bf16[16,80,128]{2,1,0:T(8,128)(2,1)S(1)}, u32[]{:S(2)}, u32[]{:S(2)}) %all-to-all-start.1) | async-done | bytes 327712 | tf_op jit(solution)/shard_map/all_to_all | solution.py:290
  59.7 1.0 %shard_map.95 = bf16[8,1024]{1,0:T(8,128)(2,1)} custom-call(bf16[16,80,128]{2,1,0:T(8,128)(2,1)S(1)} %all-to-all-done.1.got_ref, f32[64,128]{1,0:T(8,128)S(1)} %get-tuple-element.11.own_ref, f32[8,128]{1,0:T(8,128)S(1)} %get-tuple-element.12.own_stats_ref), custom_call_target="tpu_custom_call" | custom-call | flops 1000000000 | tf_op jit(solution)/shard_map/pallas_call | solution.py:297
Async XLA Ops:
  0.0 12.9 %copy-start = (bf16[8,128,512]{2,1,0:T(8,128)(2,1)S(1)}, bf16[8,128,512]{2,1,0:T(8,128)(2,1)}, u32[]{:S(2)}) copy-start(bf16[8,128,512]{2,1,0:T(8,128)(2,1)} %wuk_ref.1) | copy-start | bytes 3145732
  0.0 0.8 %copy-start.3 = (bf16[8,8,192]{2,1,0:T(8,128)(2,1)S(1)}, bf16[8,8,192]{2,1,0:T(8,128)(2,1)}, u32[]{:S(2)}) copy-start(bf16[8,8,192]{2,1,0:T(8,128)(2,1)} %queries_ref.1) | copy-start | bytes 73732
  0.8 12.1 %copy-start.4 = (bf16[8,32]{1,0:T(8,128)(2,1)S(1)}, bf16[8,32]{1,0:T(8,128)(2,1)}, u32[]{:S(2)}) copy-start(bf16[8,32]{1,0:T(8,128)(2,1)} %latent_ref.1) | copy-start | bytes 1540
  0.9 12.1 %copy-start.6 = (bf16[32]{0:T(256)(128)(2,1)S(1)}, bf16[32]{0:T(256)(128)(2,1)}, u32[]{:S(2)}) copy-start(bf16[32]{0:T(256)(128)(2,1)} %param.15) | copy-start | bytes 196
  1.7 18.1 %all-to-all-start = ((bf16[16,64,192]{2,1,0:T(8,128)(2,1)}), bf16[16,64,192]{2,1,0:T(8,128)(2,1)S(1)}, u32[]{:S(2)}, u32[]{:S(2)}) async-start(bf16[16,64,192]{2,1,0:T(8,128)(2,1)} %shard_map.91.q_ref), calls=%async_computation | async-start | bytes 1048576 | tf_op jit(solution)/shard_map/all_to_all | solution.py:270
  11.0 23.6 %collective-permute-start = (bf16[576,1024]{1,0:T(8,128)(2,1)}, bf16[576,1024]{1,0:T(8,128)(2,1)}, u32[]{:S(2)}, u32[]{:S(2)}) collective-permute-start(bf16[576,1024]{1,0:T(8,128)(2,1)} %bitcast.ka_hbm), channel_id=1, source_target_pairs={{0,16},{16,0},{1,17},{17,1},{2,18},{18,2},{3,19},{19,3},{4,20},{20... | collective-permute-start | bytes 3538952 | tf_op jit(solution)/shard_map/ppermute | solution.py:272
  19.8 14.8 %copy-start.8 = (bf16[16,64,192]{2,1,0:T(8,128)(2,1)}, bf16[16,64,192]{2,1,0:T(8,128)(2,1)S(1)}, u32[]{:S(2)}) copy-start(bf16[16,64,192]{2,1,0:T(8,128)(2,1)S(1)} %all-to-all-done.q_hbm) | copy-start | bytes 1179652
  19.8 27.3 %all-to-all-start.2 = ((bf16[16,4,128]{2,1,0:T(4,128)(2,1)}), bf16[16,4,128]{2,1,0:T(4,128)(2,1)S(1)}, u32[]{:S(2)}, u32[]{:S(2)}) async-start(bf16[16,4,128]{2,1,0:T(4,128)(2,1)} %get-tuple-element.10), calls=%async_computation.2 | async-start | bytes 32768 | tf_op jit(solution)/shard_map/all_to_all | solution.py:273
  34.6 17.3 %copy-start.1 = (bf16[8,512,128]{2,1,0:T(8,128)(2,1)S(1)}, bf16[8,512,128]{2,1,0:T(8,128)(2,1)}, u32[]{:S(2)}) copy-start(bf16[8,512,128]{2,1,0:T(8,128)(2,1)} %wuv_ref.1) | copy-start | bytes 3145732
  34.6 17.3 %copy-start.2 = (bf16[2,256,576]{1,2,0:T(8,128)(2,1)S(1)}, bf16[2,256,576]{1,2,0:T(8,128)(2,1)}, u32[]{:S(2)}) copy-start(bf16[2,256,576]{1,2,0:T(8,128)(2,1)} %param.11) | copy-start | bytes 1769476
  34.6 17.3 %copy-start.5 = (bf16[8,64]{1,0:T(8,128)(2,1)S(1)}, bf16[8,64]{1,0:T(8,128)(2,1)}, u32[]{:S(2)}) copy-start(bf16[8,64]{1,0:T(8,128)(2,1)} %rope_ref.1) | copy-start | bytes 3076
  34.6 17.3 %copy-start.7 = (s32[2]{0:T(128)S(1)}, s32[2]{0:T(128)}, u32[]{:S(2)}) copy-start(s32[2]{0:T(128)} %lengths_ref.1) | copy-start | bytes 28
  47.1 12.6 %all-to-all-start.1 = ((bf16[16,80,128]{2,1,0:T(8,128)(2,1)}), bf16[16,80,128]{2,1,0:T(8,128)(2,1)S(1)}, u32[]{:S(2)}, u32[]{:S(2)}) async-start(bf16[16,80,128]{2,1,0:T(8,128)(2,1)} %shard_map.92), calls=%async_computation.1 | async-start | bytes 655360 | tf_op jit(solution)/shard_map/all_to_all | solution.py:290

commit v3 on v2

v3 whole, which is shorter than its diff:
```python
import functools

import jax
import jax.numpy as jnp
from jax import lax
from jax.experimental import pallas as pl
from jax.experimental.pallas import tpu as pltpu
from jax.sharding import Mesh
from jax.sharding import PartitionSpec as P

eps = 1e-06
LOG2E = 1.4426950408889634
CHIPS = 16
PLANE = ("y", "x")
F32 = jnp.float32
BF16 = jnp.bfloat16
VMEM = pltpu.VMEM
NT = (((1,), (1,)), ((), ()))


def split3(value):
    high = value.astype(BF16).astype(F32)
    rest = value - high
    middle = rest.astype(BF16).astype(F32)
    return high, middle, (rest - middle).astype(BF16).astype(F32)


def queries_kernel(queries_ref, latent_ref, gain_ref, sent_ref):
    by_head = jnp.swapaxes(queries_ref[...].astype(F32), 0, 1)
    rows = by_head.reshape(64, by_head.shape[2])
    gain = jnp.concatenate([gain_ref[...].astype(F32), jnp.zeros((7, 32), F32)], 0)
    extra = jnp.concatenate([latent_ref[...].astype(F32), gain], 1)
    extra = jnp.concatenate([extra, jnp.zeros((56, 64), F32)], 0)
    rows = jnp.concatenate([rows, extra], 1).astype(BF16)
    for chip in range(CHIPS):
        sent_ref[chip] = rows


def own_kernel(width, q_ref, wuk_ref, full_ref):
    nope = wuk_ref.shape[1]
    q = q_ref[0]
    parts = []
    for pair in range(4):
        two = q[16 * pair : 16 * pair + 16, :nope]
        first = jnp.dot(two, wuk_ref[2 * pair], preferred_element_type=F32)
        second = jnp.dot(two, wuk_ref[2 * pair + 1], preferred_element_type=F32)
        parts += [first[:8], second[8:]]
    absorbed = jnp.concatenate(parts, 0)
    full_ref[...] = jnp.concatenate([absorbed, q[:, nope:width].astype(F32)], -1).astype(BF16)


def main_kernel(
    width,
    q_hbm,
    ka_hbm,
    kb_hbm,
    wuk_hbm,
    wuv_hbm,
    out_ref,
    stats_ref,
    q_ref,
    ka_ref,
    kb_ref,
    wuk_ref,
    wuv_ref,
    sems,
):
    scale = float(width) ** (-0.5)
    copies = [
        pltpu.make_async_copy(source, target, sems.at[i])
        for i, (source, target) in enumerate(
            [
                (q_hbm, q_ref),
                (wuk_hbm.at[:2], wuk_ref.at[:2]),
                (ka_hbm, ka_ref),
                (wuk_hbm.at[2:], wuk_ref.at[2:]),
                (kb_hbm, kb_ref),
                (wuv_hbm, wuv_ref),
            ]
        )
    ]
    for copy in copies:
        copy.start()
    nope, latent = wuk_ref.shape[1:]

    def absorb(pair):
        both = q_ref[:, 16 * pair : 16 * pair + 16, :].astype(F32).reshape(CHIPS, 2, 8, -1)
        fulls = []
        for j in range(2):
            one = both[:, j].reshape(128, -1).astype(BF16)
            absorbed = jnp.dot(
                one[:, :nope], wuk_ref[2 * pair + j], preferred_element_type=F32
            ).astype(BF16)
            fulls.append(jnp.concatenate([absorbed, one[:, nope:width]], -1))
        return fulls

    copies[0].wait()
    copies[1].wait()
    fulls = absorb(0)
    copies[2].wait()
    copies[3].wait()
    for pair in range(1, 4):
        fulls += absorb(pair)
    full = jnp.concatenate(fulls, 0)

    half = ka_ref.shape[1] // 2
    blocks = [(keys, i * half) for keys in (ka_ref, kb_ref) for i in range(2)]

    def score(keys, at):
        return jnp.dot(full, keys[:, at : at + half], preferred_element_type=F32)

    scores = score(*blocks[0])
    peak = None
    for i, (keys, at) in enumerate(blocks):
        if i == 0:
            copies[4].wait()
            copies[5].wait()
        later = score(*blocks[i + 1]) if i < 3 else None
        top = jnp.max(scores, -1, keepdims=True)
        top = top if peak is None else jnp.maximum(peak, top)
        expd = jnp.exp2((scores - top) * (scale * LOG2E))
        part = lax.dot_general(
            expd.astype(BF16), keys[:latent, at : at + half], NT, preferred_element_type=F32
        )
        if peak is None:
            mass, acc = jnp.sum(expd, -1, keepdims=True), part
        else:
            fade = jnp.exp2((peak - top) * (scale * LOG2E))
            mass = mass * fade + jnp.sum(expd, -1, keepdims=True)
            acc = acc * fade + part
        peak, scores = top, later

    attn = (acc / mass).astype(BF16)
    lane = lax.broadcasted_iota(jnp.int32, (128, 128), 1)
    stats = jnp.zeros((128, 128), F32)
    for pair in range(4):
        values = []
        for j in range(2):
            head = 2 * pair + j
            here = slice(128 * head, 128 * head + 128)
            values.append(
                jnp.dot(attn[here], wuv_ref[head], preferred_element_type=F32).reshape(
                    CHIPS, 8, 128
                )
            )
            for k, piece in enumerate(split3(peak[here]) + split3(mass[here])):
                stats = jnp.where(lane == 8 * k + head, piece, stats)
        out_ref[:, 16 * pair : 16 * pair + 16, :] = jnp.concatenate(values, 1).astype(BF16)
    stats_ref[...] = stats.reshape(CHIPS, 8, 128)


def attach_kernel(values_ref, stats_ref, moved_ref, out_ref):
    moved = moved_ref[...].astype(F32)[:, :8, :].reshape(128, 128)
    moved = pltpu.roll(moved, 64, 1).reshape(CHIPS, 8, 128)
    out_ref[:, :64, :] = values_ref[...]
    out_ref[:, 64:80, :] = jnp.concatenate([stats_ref[...], moved], 1).astype(BF16)


def attend(scale, full, blocks, wuv_ref):
    latent = wuv_ref.shape[1]
    scores = []
    for live, keys in blocks:
        raw = jnp.dot(full, keys, preferred_element_type=F32)
        scores.append(jnp.where(live, raw, -jnp.inf))
    peak = functools.reduce(jnp.maximum, [jnp.max(s, -1, keepdims=True) for s in scores])
    mass, acc = 0.0, 0.0
    for s, (_, keys) in zip(scores, blocks):
        p = jnp.exp2((s - peak) * (scale * LOG2E))
        mass = mass + jnp.sum(p, -1, keepdims=True)
        acc = acc + lax.dot_general(
            p.astype(BF16), keys[:latent], NT, preferred_element_type=F32
        )
    attn = (acc / mass).astype(BF16)
    lane = lax.broadcasted_iota(jnp.int32, (8, 128), 1)
    peaks = masses = jnp.zeros((8, 128), F32)
    values = []
    for pair in range(4):
        two = attn[16 * pair : 16 * pair + 16]
        first = jnp.dot(two, wuv_ref[2 * pair], preferred_element_type=F32)
        second = jnp.dot(two, wuv_ref[2 * pair + 1], preferred_element_type=F32)
        values += [first[:8], second[8:]]
    for head in range(8):
        here = slice(8 * head, 8 * head + 8)
        peaks = jnp.where(lane == head, peak[here], peaks)
        masses = jnp.where(lane == head, mass[here], masses)
    return values, peaks, masses


def suffix_kernel(scale, full_ref, suffix_ref, lengths_ref, wuv_ref, out_ref, stats_ref):
    gen = suffix_ref.shape[2]
    row = lax.broadcasted_iota(jnp.int32, (64, gen), 0) % 8
    col = lax.broadcasted_iota(jnp.int32, (64, gen), 1)
    blocks = [
        ((row // 4 == sample) & (col < lengths_ref[sample]), suffix_ref[sample])
        for sample in range(2)
    ]
    values, peaks, masses = attend(scale, full_ref[...], blocks, wuv_ref)
    out_ref[...] = jnp.concatenate(values, 0)
    stats_ref[...] = jnp.concatenate([peaks, masses], 0)


def combine_kernel(
    scale, got_ref, suffix_ref, suffix_stats_ref, full_ref, rope_ref, wuv_ref, out_ref
):
    place = lax.axis_index("z")
    lane = lax.broadcasted_iota(jnp.int32, (8, 128), 1) // 32
    latents, gains = [], []
    for g in range(4):
        latent, gain = 0.0, 0.0
        for j in range(4):
            chip = (place - (4 * g + j)) & 15
            piece = got_ref[chip, 64:80, :].astype(F32)[8:]
            one = jnp.where(lane == 0, piece, 0.0)
            latent = latent + (pltpu.roll(one, 32 * j, 1) if j else one)
            one = jnp.where(lane == 1, piece, 0.0)
            shift = (32 * (j - 1)) % 128
            gain = gain + (pltpu.roll(one, shift, 1) if shift else one)
        latents.append(latent)
        gains.append(gain)
    plain, gain = jnp.concatenate(latents, -1), jnp.concatenate(gains, -1)[:1]
    square = jnp.sum(plain * plain, -1, keepdims=True) / plain.shape[1]
    normed = plain * lax.rsqrt(square + eps) * gain
    fresh = jnp.concatenate([normed, rope_ref[...].astype(F32)], -1)
    fresh = jnp.concatenate([fresh, jnp.zeros((120, fresh.shape[1]), F32)], 0)
    row = lax.broadcasted_iota(jnp.int32, (64, 128), 0) % 8
    col = lax.broadcasted_iota(jnp.int32, (64, 128), 1)
    live = (col < 8) & (col // 4 == row // 4) & (col <= row)
    fresh_values, fresh_peak, fresh_mass = attend(
        scale, full_ref[...], [(live, fresh.T.astype(BF16))], wuv_ref
    )

    raw = got_ref[:, 64:80, :].astype(F32)[:, :8, :].reshape(128, 128)

    def lanes(k):
        return raw if k == 0 else pltpu.roll(raw, 128 - 8 * k, 1)

    peaks = (lanes(0) + lanes(1) + lanes(2)).reshape(CHIPS, 8, 128)
    masses = (lanes(3) + lanes(4) + lanes(5)).reshape(CHIPS, 8, 128)
    suffix_peak, suffix_mass = suffix_stats_ref[:8], suffix_stats_ref[8:]
    peak = jnp.maximum(jnp.max(peaks, 0), jnp.maximum(suffix_peak, fresh_peak))
    weights = jnp.exp2((peaks - peak[None]) * (scale * LOG2E)) * masses
    suffix_weight = jnp.exp2((suffix_peak - peak) * (scale * LOG2E)) * suffix_mass
    fresh_weight = jnp.exp2((fresh_peak - peak) * (scale * LOG2E)) * fresh_mass
    inverse = 1.0 / (jnp.sum(weights, 0) + suffix_weight + fresh_weight)
    for pair in range(4):
        got = got_ref[:, 16 * pair : 16 * pair + 16, :].astype(F32)
        for j in range(2):
            head = 2 * pair + j
            this = slice(head, head + 1)
            total = suffix_weight[:, this] * suffix_ref[8 * head : 8 * head + 8, :]
            total = total + fresh_weight[:, this] * fresh_values[head]
            for chip in range(CHIPS):
                total = total + weights[chip, :, this] * got[chip, 8 * j : 8 * j + 8, :]
            total = total * inverse[:, this]
            out_ref[:, 128 * head : 128 * head + 128] = total.astype(BF16)


def call(kernel, outs, n_in, smem=(), hbm=(), scratch=(), cost=1, mib=24):
    spaces = [pltpu.SMEM if i in smem else pl.ANY if i in hbm else VMEM for i in range(n_in)]
    return pl.pallas_call(
        kernel,
        out_shape=outs,
        in_specs=[pl.BlockSpec(memory_space=space) for space in spaces],
        out_specs=jax.tree.map(lambda _: pl.BlockSpec(memory_space=VMEM), outs),
        scratch_shapes=scratch,
        compiler_params=pltpu.CompilerParams(vmem_limit_bytes=mib * 1024 * 1024),
        cost_estimate=pl.CostEstimate(
            flops=cost * 10**9, transcendentals=0, bytes_accessed=0
        ),
    )


def per_device(
    queries, prompt_cache, suffix_cache, gen_lengths, new_latent, new_rope, latent_gain, w_uk, w_uv
):
    width = queries.shape[2]
    scale = float(width) ** (-0.5)
    sent = call(
        queries_kernel, jax.ShapeDtypeStruct((CHIPS, 64, 256), BF16), 3, mib=62
    )(queries, new_latent, latent_gain[None])
    gathered = lax.all_to_all(sent, PLANE, 0, 0, tiled=True)
    keys = prompt_cache.T
    other = lax.ppermute(keys, "core", [(0, 1), (1, 0)])
    full = call(
        functools.partial(own_kernel, width),
        jax.ShapeDtypeStruct((64, keys.shape[0]), BF16),
        2,
        cost=30,
    )(sent, w_uk)

    devices = [(p, core, z) for p in range(CHIPS) for core in range(2) for z in range(16)]
    moves = [
        ((2 * p + core) * 16 + z, (2 * p + core) * 16 + (z + p) % 16) for p, core, z in devices
    ]
    moved = lax.ppermute(gathered[:, :16, 128:], ("y", "x", "core", "z"), moves)

    values, stats = call(
        functools.partial(main_kernel, width),
        (
            jax.ShapeDtypeStruct((CHIPS, 64, 128), BF16),
            jax.ShapeDtypeStruct((CHIPS, 8, 128), F32),
        ),
        5,
        hbm=(0, 1, 2, 3, 4),
        scratch=[
            VMEM(gathered.shape, BF16),
            VMEM(keys.shape, BF16),
            VMEM(keys.shape, BF16),
            VMEM(w_uk.shape, BF16),
            VMEM(w_uv.shape, BF16),
            pltpu.SemaphoreType.DMA((6,)),
        ],
        cost=8,
        mib=52,
    )(gathered, keys, other, w_uk, w_uv)
    parts = call(attach_kernel, jax.ShapeDtypeStruct((CHIPS, 80, 128), BF16), 3)(
        values, stats, moved
    )
    got = lax.all_to_all(parts, PLANE, 0, 0, tiled=True)
    suffix, suffix_stats = call(
        functools.partial(suffix_kernel, scale),
        (jax.ShapeDtypeStruct((64, 128), F32), jax.ShapeDtypeStruct((16, 128), F32)),
        4,
        smem=(2,),
        cost=5,
    )(full, jnp.swapaxes(suffix_cache, 1, 2), gen_lengths, w_uv)
    return call(
        functools.partial(combine_kernel, scale), jax.ShapeDtypeStruct((8, 1024), BF16), 6
    )(got, suffix, suffix_stats, full, new_rope, w_uv)


def solution(mesh):
    fine = Mesh(mesh.devices.reshape(4, 4, 2, 16), ("y", "x", "core", "z"))
    seq = ("y", "x", "core")
    return jax.shard_map(
        per_device,
        mesh=fine,
        in_specs=(
            P(seq, "z", None),
            P(seq, None),
            P(seq, None, None),
            P(seq),
            P(seq, "z"),
            P(seq, None),
            P("z"),
            P("z", None, None),
            P("z", None, None),
        ),
        out_specs=P(seq, "z"),
        check_vma=False,
    )
```

time: 61.1 us -> 57.8 us (0.946)
  the two profiles are of different devices: /device:TPU:2 before, /device:TPU:32 now
where the time goes in v3:
time: 57.8 us; the launch traced here: 57.4 us
  starting transfers between devices  26 us (45%)
  waiting for transfers between devices  16.1 us (28%)
  Pallas kernels  14 us (24%)
  local copies, waits for them, and re-layouts  1.08 us (2%)
    all_to_all x1, starting transfers between devices, per_device(): got = lax.all_to_all(parts, PLANE, 0, 0, tiled=True)  16.4 us
    pallas_call x1, Pallas kernels, per_device(): call(functools.partial(main_kernel, width), (jax.ShapeDtypeStruct((CHIPS,...  8.42 us
    all_to_all x1, waiting for transfers between devices, per_device(): gathered = lax.all_to_all(sent, PLANE, 0, 0, tiled=True)  8.33 us
    all_to_all x1, waiting for transfers between devices, per_device(): got = lax.all_to_all(parts, PLANE, 0, 0, tiled=True)  7.73 us
    all_to_all x1, starting transfers between devices, per_device(): gathered = lax.all_to_all(sent, PLANE, 0, 0, tiled=True)  7.03 us
    ppermute x1, starting transfers between devices, per_device(): other = lax.ppermute(keys, 'core', [(0, 1), (1, 0)])  1.92 us
    pallas_call x1, Pallas kernels, per_device(): call(queries_kernel, jax.ShapeDtypeStruct((CHIPS, 64, 256), BF16), 3, mib...  1.84 us
    pallas_call x1, Pallas kernels, per_device(): call(functools.partial(combine_kernel, scale), jax.ShapeDtypeStruct((8, 1...  1.52 us
  transfers between devices with their start and end apart: 4, of which 2 were waited for; matrix products, arithmetic and copies ran while one was open for 0% of the time, Pallas kernels for 17%

profile of v3, /device:TPU:32, one launch (start us, length us, event | category | flops | bytes accessed | tf_op | source)
XLA Modules:
  0.0 57.4 jit_solution(16294315426503357624)
XLA Ops:
  0.0 0.0 copy-start.1
  0.0 1.8 %shard_map.91.q_ref = bf16[16,64,256]{2,1,0:T(8,128)(2,1)} custom-call(bf16[8,8,192]{2,1,0:T(8,128)(2,1)} %queries_ref.1, bf16[8,32]{1,0:T(8,128)(2,1)} %latent_ref.1, bf16[1,32]{1,0:T(2,128)(2,1)} %bitcast.6), custom_call_target="tpu_custom_call" | custom-call | flops 1000000000 | tf_op jit(solution)/shard_map/pallas_call | solution.py:278
  1.8 7.0 %all-to-all-start = ((bf16[16,64,256]{2,1,0:T(8,128)(2,1)}), bf16[16,64,256]{2,1,0:T(8,128)(2,1)S(1)}, u32[]{:S(2)}, u32[]{:S(2)}) async-start(bf16[16,64,256]{2,1,0:T(8,128)(2,1)} %shard_map.91.q_ref), calls=%async_computation | async-start | bytes 1048576 | tf_op jit(solution)/shard_map/all_to_all | solution.py:281
  8.9 1.9 %collective-permute-start = (bf16[576,1024]{1,0:T(8,128)(2,1)}, bf16[576,1024]{1,0:T(8,128)(2,1)}, u32[]{:S(2)}, u32[]{:S(2)}) collective-permute-start(bf16[576,1024]{1,0:T(8,128)(2,1)} %bitcast.4), channel_id=1, source_target_pairs={{0,16},{16,0},{1,17},{17,1},{2,18},{18,2},{3,19},{19,3},{4,20},{20... | collective-permute-start | bytes 3538952 | tf_op jit(solution)/shard_map/ppermute | solution.py:283
  10.8 0.0 copy-done.1
  10.8 0.0 copy-start
  10.8 1.0 %copy-done = bf16[16,64,256]{2,1,0:T(8,128)(2,1)S(1)} copy-done((bf16[16,64,256]{2,1,0:T(8,128)(2,1)S(1)}, bf16[16,64,256]{2,1,0:T(8,128)(2,1)}, u32[]{:S(2)}) %copy-start) | copy-done | bytes 524312
  11.9 0.2 shard_map.94.full_ref
  12.1 8.3 %all-to-all-done.q_hbm = bf16[16,64,256]{2,1,0:T(8,128)(2,1)S(1)} async-done(((bf16[16,64,256]{2,1,0:T(8,128)(2,1)}), bf16[16,64,256]{2,1,0:T(8,128)(2,1)S(1)}, u32[]{:S(2)}, u32[]{:S(2)}) %all-to-all-start) | async-done | bytes 524320 | tf_op jit(solution)/shard_map/all_to_all | solution.py:281
  20.4 0.7 %collective-permute-start.1 = (bf16[16,16,128]{2,1,0:T(8,128)(2,1)S(1)}, bf16[16,16,128]{2,1,0:T(8,128)(2,1)S(1)}, u32[]{:S(2)}, u32[]{:S(2)}) collective-permute-start(bf16[16,16,128]{2,1,0:T(8,128)(2,1)S(1)} %slice.4), channel_id=1, source_target_pairs={{0,0},{1,1},{2,2},{3,3},{4,4},{5,5},{6,6},{7,7},{8,8},{9,9},{10,10... | collective-permute-start | bytes 196616 | tf_op jit(solution)/shard_map/ppermute | solution.py:295
  21.1 0.0 collective-permute-done.kb_hbm
  21.1 8.4 %shard_map.92 = (bf16[16,64,128]{2,1,0:T(8,128)(2,1)S(1)}, f32[16,8,128]{2,1,0:T(8,128)S(1)}) custom-call(bf16[16,64,256]{2,1,0:T(8,128)(2,1)S(1)} %all-to-all-done.q_hbm, bf16[576,1024]{1,0:T(8,128)(2,1)} %bitcast.5, bf16[576,1024]{1,0:T(8,128)(2,1)} %collective-permute-done.kb_hbm, bf16[8,128,512]{2,1,0:T(8,128)(2,1)S(1)} %copy-done.1, ...), custom_call_target="tpu_custom_call" | custom-call | flops 8000000000 | tf_op jit(solution)/shard_map/pallas_call | solution.py:297
  29.5 0.0 collective-permute-done.1.moved_ref
  29.6 0.0 copy-start.2
  29.6 0.0 copy-start.3
  29.6 0.0 copy-start.5
  29.6 0.8 %shard_map.93 = bf16[16,80,128]{2,1,0:T(8,128)(2,1)} custom-call(bf16[16,64,128]{2,1,0:T(8,128)(2,1)S(1)} %get-tuple-element.9.values_ref, f32[16,8,128]{2,1,0:T(8,128)S(1)} %get-tuple-element.10.stats_ref, bf16[16,16,128]{2,1,0:T(8,128)(2,1)S(1)} %collective-permute-done.1.moved_ref), custom_call_target="tpu_custom_call" | custom-call | flops 1000000000 | tf_op jit(solution)/shard_map/pallas_call | solution.py:316
  30.4 16.4 %all-to-all-start.1 = ((bf16[16,80,128]{2,1,0:T(8,128)(2,1)}), bf16[16,80,128]{2,1,0:T(8,128)(2,1)S(1)}, u32[]{:S(2)}, u32[]{:S(2)}) async-start(bf16[16,80,128]{2,1,0:T(8,128)(2,1)} %shard_map.93), calls=%async_computation.1 | async-start | bytes 655360 | tf_op jit(solution)/shard_map/all_to_all | solution.py:319
  46.8 0.0 copy-done.2
  46.8 0.0 copy-done.3
  46.8 0.0 copy-done.5
  46.8 0.0 copy-start.4
  46.9 1.3 %shard_map.95 = (f32[64,128]{1,0:T(8,128)S(1)}, f32[16,128]{1,0:T(8,128)S(1)}) custom-call(bf16[64,576]{1,0:T(8,128)(2,1)S(1)} %shard_map.94.full_ref, bf16[2,576,256]{2,1,0:T(8,128)(2,1)S(1)} %bitcast.3, s32[2]{0:T(128)S(1)} %copy-done.5, bf16[8,512,128]{2,1,0:T(8,128)(2,1)S(1)} %copy-done.2), custom_call_target="tpu_custom_call" | custom-call | flops 5000000000 | tf_op jit(solution)/shard_map/pallas_call | solution.py:320
  48.1 7.7 %all-to-all-done.1.got_ref = bf16[16,80,128]{2,1,0:T(8,128)(2,1)S(1)} async-done(((bf16[16,80,128]{2,1,0:T(8,128)(2,1)}), bf16[16,80,128]{2,1,0:T(8,128)(2,1)S(1)}, u32[]{:S(2)}, u32[]{:S(2)}) %all-to-all-start.1) | async-done | bytes 327712 | tf_op jit(solution)/shard_map/all_to_all | solution.py:319
  55.9 0.0 copy-done.4
  55.9 1.5 %shard_map.96 = bf16[8,1024]{1,0:T(8,128)(2,1)} custom-call(bf16[16,80,128]{2,1,0:T(8,128)(2,1)S(1)} %all-to-all-done.1.got_ref, f32[64,128]{1,0:T(8,128)S(1)} %get-tuple-element.11.suffix_ref, f32[16,128]{1,0:T(8,128)S(1)} %get-tuple-element.12.suffix_stats_ref, bf16[64,576]{1,0:T(8,128)(2,1)S(1)} %shard_map.94.full_ref, bf16[8,64]{1,0:T(8,128)(2,1)S(1)} %copy-done.4, ...), custom_call_target="tpu_custom_call" | custom-call | flops 1000000000 | tf_op jit(solution)/shard_map/pallas_call | solution.py:327
  (1 shorter events, 0.0 us)
Async XLA Ops:
  0.0 10.8 %copy-start.1 = (bf16[8,128,512]{2,1,0:T(8,128)(2,1)S(1)}, bf16[8,128,512]{2,1,0:T(8,128)(2,1)}, u32[]{:S(2)}) copy-start(bf16[8,128,512]{2,1,0:T(8,128)(2,1)} %wuk_ref.1) | copy-start | bytes 3145732
  1.8 18.6 %all-to-all-start = ((bf16[16,64,256]{2,1,0:T(8,128)(2,1)}), bf16[16,64,256]{2,1,0:T(8,128)(2,1)S(1)}, u32[]{:S(2)}, u32[]{:S(2)}) async-start(bf16[16,64,256]{2,1,0:T(8,128)(2,1)} %shard_map.91.q_ref), calls=%async_computation | async-start | bytes 1048576 | tf_op jit(solution)/shard_map/all_to_all | solution.py:281
  8.9 12.2 %collective-permute-start = (bf16[576,1024]{1,0:T(8,128)(2,1)}, bf16[576,1024]{1,0:T(8,128)(2,1)}, u32[]{:S(2)}, u32[]{:S(2)}) collective-permute-start(bf16[576,1024]{1,0:T(8,128)(2,1)} %bitcast.4), channel_id=1, source_target_pairs={{0,16},{16,0},{1,17},{17,1},{2,18},{18,2},{3,19},{19,3},{4,20},{20... | collective-permute-start | bytes 3538952 | tf_op jit(solution)/shard_map/ppermute | solution.py:283
  10.8 1.0 %copy-start = (bf16[16,64,256]{2,1,0:T(8,128)(2,1)S(1)}, bf16[16,64,256]{2,1,0:T(8,128)(2,1)}, u32[]{:S(2)}) copy-start(bf16[16,64,256]{2,1,0:T(8,128)(2,1)} %shard_map.91.q_ref) | copy-start | bytes 1572868
  20.4 9.1 %collective-permute-start.1 = (bf16[16,16,128]{2,1,0:T(8,128)(2,1)S(1)}, bf16[16,16,128]{2,1,0:T(8,128)(2,1)S(1)}, u32[]{:S(2)}, u32[]{:S(2)}) collective-permute-start(bf16[16,16,128]{2,1,0:T(8,128)(2,1)S(1)} %slice.4), channel_id=1, source_target_pairs={{0,0},{1,1},{2,2},{3,3},{4,4},{5,5},{6,6},{7,7},{8,8},{9,9},{10,10... | collective-permute-start | bytes 196616 | tf_op jit(solution)/shard_map/ppermute | solution.py:295
  29.6 17.3 %copy-start.2 = (bf16[8,512,128]{2,1,0:T(8,128)(2,1)S(1)}, bf16[8,512,128]{2,1,0:T(8,128)(2,1)}, u32[]{:S(2)}) copy-start(bf16[8,512,128]{2,1,0:T(8,128)(2,1)} %wuv_ref.3) | copy-start | bytes 3145732
  29.6 17.3 %copy-start.3 = (bf16[2,256,576]{1,2,0:T(8,128)(2,1)S(1)}, bf16[2,256,576]{1,2,0:T(8,128)(2,1)}, u32[]{:S(2)}) copy-start(bf16[2,256,576]{1,2,0:T(8,128)(2,1)} %param.11) | copy-start | bytes 1769476
  29.6 17.3 %copy-start.5 = (s32[2]{0:T(128)S(1)}, s32[2]{0:T(128)}, u32[]{:S(2)}) copy-start(s32[2]{0:T(128)} %lengths_ref.1) | copy-start | bytes 28
  30.4 25.5 %all-to-all-start.1 = ((bf16[16,80,128]{2,1,0:T(8,128)(2,1)}), bf16[16,80,128]{2,1,0:T(8,128)(2,1)S(1)}, u32[]{:S(2)}, u32[]{:S(2)}) async-start(bf16[16,80,128]{2,1,0:T(8,128)(2,1)} %shard_map.93), calls=%async_computation.1 | async-start | bytes 655360 | tf_op jit(solution)/shard_map/all_to_all | solution.py:319
  46.8 9.0 %copy-start.4 = (bf16[8,64]{1,0:T(8,128)(2,1)S(1)}, bf16[8,64]{1,0:T(8,128)(2,1)}, u32[]{:S(2)}) copy-start(bf16[8,64]{1,0:T(8,128)(2,1)} %rope_ref.1) | copy-start | bytes 3076

commit v4 on v3

--- a/solution.py
+++ b/solution.py
@@ -12,6 +12,9 @@
 LOG2E = 1.4426950408889634
 CHIPS = 16
 PLANE = ("y", "x")
+ORDER = sorted(
+    range(CHIPS), key=lambda p: (abs(p // 4 - 2) + min((p - 2) % 4, (2 - p) % 4), p)
+)
 F32 = jnp.float32
 BF16 = jnp.bfloat16
 VMEM = pltpu.VMEM
@@ -208,7 +211,7 @@
     for g in range(4):
         latent, gain = 0.0, 0.0
         for j in range(4):
-            chip = (place - (4 * g + j)) & 15
+            chip = ((place - (4 * g + j)) & 15) ^ 8
             piece = got_ref[chip, 64:80, :].astype(F32)[8:]
             one = jnp.where(lane == 0, piece, 0.0)
             latent = latent + (pltpu.roll(one, 32 * j, 1) if j else one)
@@ -278,7 +281,7 @@
     sent = call(
         queries_kernel, jax.ShapeDtypeStruct((CHIPS, 64, 256), BF16), 3, mib=62
     )(queries, new_latent, latent_gain[None])
-    gathered = lax.all_to_all(sent, PLANE, 0, 0, tiled=True)
+    gathered = lax.all_to_all(sent, PLANE, 0, 0, axis_index_groups=[ORDER], tiled=True)
     keys = prompt_cache.T
     other = lax.ppermute(keys, "core", [(0, 1), (1, 0)])
     full = call(
@@ -288,9 +291,11 @@
         cost=30,
     )(sent, w_uk)
 
-    devices = [(p, core, z) for p in range(CHIPS) for core in range(2) for z in range(16)]
     moves = [
-        ((2 * p + core) * 16 + z, (2 * p + core) * 16 + (z + p) % 16) for p, core, z in devices
+        ((2 * p + core) * 16 + z, (2 * p + core) * 16 + (z + (8 ^ k)) % 16)
+        for k, p in enumerate(ORDER)
+        for core in range(2)
+        for z in range(16)
     ]
     moved = lax.ppermute(gathered[:, :16, 128:], ("y", "x", "core", "z"), moves)
 
@@ -316,7 +321,7 @@
     parts = call(attach_kernel, jax.ShapeDtypeStruct((CHIPS, 80, 128), BF16), 3)(
         values, stats, moved
     )
-    got = lax.all_to_all(parts, PLANE, 0, 0, tiled=True)
+    got = lax.all_to_all(parts, PLANE, 0, 0, axis_index_groups=[ORDER], tiled=True)
     suffix, suffix_stats = call(
         functools.partial(suffix_kernel, scale),
         (jax.ShapeDtypeStruct((64, 128), F32), jax.ShapeDtypeStruct((16, 128), F32)),

time: 57.8 us -> 55.9 us (0.967)
  the two profiles are of different devices: /device:TPU:32 before, /device:TPU:6 now
where the time goes in v4:
time: 55.9 us; the launch traced here: 55.1 us
  starting transfers between devices  31.6 us (57%)
  Pallas kernels  14 us (25%)
  waiting for transfers between devices  8.25 us (15%)
  local copies, waits for them, and re-layouts  1.08 us (2%)
    all_to_all x1, starting transfers between devices, per_device(): lax.all_to_all(parts, PLANE, 0, 0, axis_index_groups=[ORDER], tiled=True)  12.1 us
    all_to_all x1, starting transfers between devices, per_device(): lax.all_to_all(sent, PLANE, 0, 0, axis_index_groups=[ORDER], tiled=True)  10.4 us
    pallas_call x1, Pallas kernels, per_device(): call(functools.partial(main_kernel, width), (jax.ShapeDtypeStruct((CHIPS,...  8.42 us
    ppermute x1, starting transfers between devices, per_device(): moved = lax.ppermute(gathered[:, :16, 128:], ('y', 'x', 'core', 'z'), moves)  7.25 us
    all_to_all x1, waiting for transfers between devices, per_device(): lax.all_to_all(parts, PLANE, 0, 0, axis_index_groups=[ORDER], tiled=True)  4.46 us
    all_to_all x1, waiting for transfers between devices, per_device(): lax.all_to_all(sent, PLANE, 0, 0, axis_index_groups=[ORDER], tiled=True)  3.78 us
    ppermute x1, starting transfers between devices, per_device(): other = lax.ppermute(keys, 'core', [(0, 1), (1, 0)])  1.91 us
    pallas_call x1, Pallas kernels, per_device(): call(queries_kernel, jax.ShapeDtypeStruct((CHIPS, 64, 256), BF16), 3, mib...  1.84 us
  transfers between devices with their start and end apart: 4, of which 2 were waited for; matrix products, arithmetic and copies ran while one was open for 0% of the time, Pallas kernels for 18%

profile of v4, /device:TPU:6, one launch (start us, length us, event | category | flops | bytes accessed | tf_op | source)
XLA Modules:
  0.0 55.1 jit_solution(6976935305831674700)
XLA Ops:
  0.0 0.0 copy-start.1
  0.0 1.8 %shard_map.91.q_ref = bf16[16,64,256]{2,1,0:T(8,128)(2,1)} custom-call(bf16[8,8,192]{2,1,0:T(8,128)(2,1)} %queries_ref.1, bf16[8,32]{1,0:T(8,128)(2,1)} %latent_ref.1, bf16[1,32]{1,0:T(2,128)(2,1)} %bitcast.6), custom_call_target="tpu_custom_call" | custom-call | flops 1000000000 | tf_op jit(solution)/shard_map/pallas_call | solution.py:281
  1.8 10.4 %all-to-all-start = ((bf16[16,64,256]{2,1,0:T(8,128)(2,1)}), bf16[16,64,256]{2,1,0:T(8,128)(2,1)S(1)}, u32[]{:S(2)}, u32[]{:S(2)}) async-start(bf16[16,64,256]{2,1,0:T(8,128)(2,1)} %shard_map.91.q_ref), calls=%async_computation | async-start | bytes 1048576 | tf_op jit(solution)/shard_map/all_to_all | solution.py:284
  12.2 1.9 %collective-permute-start = (bf16[576,1024]{1,0:T(8,128)(2,1)}, bf16[576,1024]{1,0:T(8,128)(2,1)}, u32[]{:S(2)}, u32[]{:S(2)}) collective-permute-start(bf16[576,1024]{1,0:T(8,128)(2,1)} %bitcast.4), channel_id=1, source_target_pairs={{0,16},{16,0},{1,17},{17,1},{2,18},{18,2},{3,19},{19,3},{4,20},{20... | collective-permute-start | bytes 3538952 | tf_op jit(solution)/shard_map/ppermute | solution.py:286
  14.2 0.0 copy-done.1
  14.2 0.0 copy-start
  14.2 1.0 %copy-done = bf16[16,64,256]{2,1,0:T(8,128)(2,1)S(1)} copy-done((bf16[16,64,256]{2,1,0:T(8,128)(2,1)S(1)}, bf16[16,64,256]{2,1,0:T(8,128)(2,1)}, u32[]{:S(2)}) %copy-start) | copy-done | bytes 524312
  15.2 0.2 shard_map.94.full_ref
  15.4 3.8 %all-to-all-done.q_hbm = bf16[16,64,256]{2,1,0:T(8,128)(2,1)S(1)} async-done(((bf16[16,64,256]{2,1,0:T(8,128)(2,1)}), bf16[16,64,256]{2,1,0:T(8,128)(2,1)S(1)}, u32[]{:S(2)}, u32[]{:S(2)}) %all-to-all-start) | async-done | bytes 524320 | tf_op jit(solution)/shard_map/all_to_all | solution.py:284
  19.2 7.3 %collective-permute-start.1 = (bf16[16,16,128]{2,1,0:T(8,128)(2,1)S(1)}, bf16[16,16,128]{2,1,0:T(8,128)(2,1)S(1)}, u32[]{:S(2)}, u32[]{:S(2)}) collective-permute-start(bf16[16,16,128]{2,1,0:T(8,128)(2,1)S(1)} %slice.4), channel_id=1, source_target_pairs={{320,328},{321,329},{322,330},{323,331},{324,332},{325,333},{326,3... | collective-permute-start | bytes 196616 | tf_op jit(solution)/shard_map/ppermute | solution.py:300
  26.5 0.0 collective-permute-done.kb_hbm
  26.5 8.4 %shard_map.92 = (bf16[16,64,128]{2,1,0:T(8,128)(2,1)S(1)}, f32[16,8,128]{2,1,0:T(8,128)S(1)}) custom-call(bf16[16,64,256]{2,1,0:T(8,128)(2,1)S(1)} %all-to-all-done.q_hbm, bf16[576,1024]{1,0:T(8,128)(2,1)} %bitcast.5, bf16[576,1024]{1,0:T(8,128)(2,1)} %collective-permute-done.kb_hbm, bf16[8,128,512]{2,1,0:T(8,128)(2,1)S(1)} %copy-done.1, ...), custom_call_target="tpu_custom_call" | custom-call | flops 8000000000 | tf_op jit(solution)/shard_map/pallas_call | solution.py:302
  34.9 0.0 collective-permute-done.1.moved_ref
  34.9 0.0 copy-start.2
  35.0 0.0 copy-start.3
  35.0 0.0 copy-start.5
  35.0 0.8 %shard_map.93 = bf16[16,80,128]{2,1,0:T(8,128)(2,1)} custom-call(bf16[16,64,128]{2,1,0:T(8,128)(2,1)S(1)} %get-tuple-element.9.values_ref, f32[16,8,128]{2,1,0:T(8,128)S(1)} %get-tuple-element.10.stats_ref, bf16[16,16,128]{2,1,0:T(8,128)(2,1)S(1)} %collective-permute-done.1.moved_ref), custom_call_target="tpu_custom_call" | custom-call | flops 1000000000 | tf_op jit(solution)/shard_map/pallas_call | solution.py:321
  35.8 12.1 %all-to-all-start.1 = ((bf16[16,80,128]{2,1,0:T(8,128)(2,1)}), bf16[16,80,128]{2,1,0:T(8,128)(2,1)S(1)}, u32[]{:S(2)}, u32[]{:S(2)}) async-start(bf16[16,80,128]{2,1,0:T(8,128)(2,1)} %shard_map.93), calls=%async_computation.1 | async-start | bytes 655360 | tf_op jit(solution)/shard_map/all_to_all | solution.py:324
  47.8 0.0 copy-done.2
  47.8 0.0 copy-done.3
  47.8 0.0 copy-done.5
  47.9 0.0 copy-start.4
  47.9 1.3 %shard_map.95 = (f32[64,128]{1,0:T(8,128)S(1)}, f32[16,128]{1,0:T(8,128)S(1)}) custom-call(bf16[64,576]{1,0:T(8,128)(2,1)S(1)} %shard_map.94.full_ref, bf16[2,576,256]{2,1,0:T(8,128)(2,1)S(1)} %bitcast.3, s32[2]{0:T(128)S(1)} %copy-done.5, bf16[8,512,128]{2,1,0:T(8,128)(2,1)S(1)} %copy-done.2), custom_call_target="tpu_custom_call" | custom-call | flops 5000000000 | tf_op jit(solution)/shard_map/pallas_call | solution.py:325
  49.1 4.5 %all-to-all-done.1.got_ref = bf16[16,80,128]{2,1,0:T(8,128)(2,1)S(1)} async-done(((bf16[16,80,128]{2,1,0:T(8,128)(2,1)}), bf16[16,80,128]{2,1,0:T(8,128)(2,1)S(1)}, u32[]{:S(2)}, u32[]{:S(2)}) %all-to-all-start.1) | async-done | bytes 327712 | tf_op jit(solution)/shard_map/all_to_all | solution.py:324
  53.6 0.0 copy-done.4
  53.6 1.5 %shard_map.96 = bf16[8,1024]{1,0:T(8,128)(2,1)} custom-call(bf16[16,80,128]{2,1,0:T(8,128)(2,1)S(1)} %all-to-all-done.1.got_ref, f32[64,128]{1,0:T(8,128)S(1)} %get-tuple-element.11.suffix_ref, f32[16,128]{1,0:T(8,128)S(1)} %get-tuple-element.12.suffix_stats_ref, bf16[64,576]{1,0:T(8,128)(2,1)S(1)} %shard_map.94.full_ref, bf16[8,64]{1,0:T(8,128)(2,1)S(1)} %copy-done.4, ...), custom_call_target="tpu_custom_call" | custom-call | flops 1000000000 | tf_op jit(solution)/shard_map/pallas_call | solution.py:332
  (1 shorter events, 0.0 us)
Async XLA Ops:
  0.0 14.2 %copy-start.1 = (bf16[8,128,512]{2,1,0:T(8,128)(2,1)S(1)}, bf16[8,128,512]{2,1,0:T(8,128)(2,1)}, u32[]{:S(2)}) copy-start(bf16[8,128,512]{2,1,0:T(8,128)(2,1)} %wuk_ref.1) | copy-start | bytes 3145732
  1.8 17.4 %all-to-all-start = ((bf16[16,64,256]{2,1,0:T(8,128)(2,1)}), bf16[16,64,256]{2,1,0:T(8,128)(2,1)S(1)}, u32[]{:S(2)}, u32[]{:S(2)}) async-start(bf16[16,64,256]{2,1,0:T(8,128)(2,1)} %shard_map.91.q_ref), calls=%async_computation | async-start | bytes 1048576 | tf_op jit(solution)/shard_map/all_to_all | solution.py:284
  12.2 14.2 %collective-permute-start = (bf16[576,1024]{1,0:T(8,128)(2,1)}, bf16[576,1024]{1,0:T(8,128)(2,1)}, u32[]{:S(2)}, u32[]{:S(2)}) collective-permute-start(bf16[576,1024]{1,0:T(8,128)(2,1)} %bitcast.4), channel_id=1, source_target_pairs={{0,16},{16,0},{1,17},{17,1},{2,18},{18,2},{3,19},{19,3},{4,20},{20... | collective-permute-start | bytes 3538952 | tf_op jit(solution)/shard_map/ppermute | solution.py:286
  14.2 1.0 %copy-start = (bf16[16,64,256]{2,1,0:T(8,128)(2,1)S(1)}, bf16[16,64,256]{2,1,0:T(8,128)(2,1)}, u32[]{:S(2)}) copy-start(bf16[16,64,256]{2,1,0:T(8,128)(2,1)} %shard_map.91.q_ref) | copy-start | bytes 1572868
  19.2 15.7 %collective-permute-start.1 = (bf16[16,16,128]{2,1,0:T(8,128)(2,1)S(1)}, bf16[16,16,128]{2,1,0:T(8,128)(2,1)S(1)}, u32[]{:S(2)}, u32[]{:S(2)}) collective-permute-start(bf16[16,16,128]{2,1,0:T(8,128)(2,1)S(1)} %slice.4), channel_id=1, source_target_pairs={{320,328},{321,329},{322,330},{323,331},{324,332},{325,333},{326,3... | collective-permute-start | bytes 196616 | tf_op jit(solution)/shard_map/ppermute | solution.py:300
  34.9 12.9 %copy-start.2 = (bf16[8,512,128]{2,1,0:T(8,128)(2,1)S(1)}, bf16[8,512,128]{2,1,0:T(8,128)(2,1)}, u32[]{:S(2)}) copy-start(bf16[8,512,128]{2,1,0:T(8,128)(2,1)} %wuv_ref.3) | copy-start | bytes 3145732
  35.0 12.9 %copy-start.3 = (bf16[2,256,576]{1,2,0:T(8,128)(2,1)S(1)}, bf16[2,256,576]{1,2,0:T(8,128)(2,1)}, u32[]{:S(2)}) copy-start(bf16[2,256,576]{1,2,0:T(8,128)(2,1)} %param.11) | copy-start | bytes 1769476
  35.0 12.9 %copy-start.5 = (s32[2]{0:T(128)S(1)}, s32[2]{0:T(128)}, u32[]{:S(2)}) copy-start(s32[2]{0:T(128)} %lengths_ref.1) | copy-start | bytes 28
  35.8 17.8 %all-to-all-start.1 = ((bf16[16,80,128]{2,1,0:T(8,128)(2,1)}), bf16[16,80,128]{2,1,0:T(8,128)(2,1)S(1)}, u32[]{:S(2)}, u32[]{:S(2)}) async-start(bf16[16,80,128]{2,1,0:T(8,128)(2,1)} %shard_map.93), calls=%async_computation.1 | async-start | bytes 655360 | tf_op jit(solution)/shard_map/all_to_all | solution.py:324
  47.9 5.8 %copy-start.4 = (bf16[8,64]{1,0:T(8,128)(2,1)S(1)}, bf16[8,64]{1,0:T(8,128)(2,1)}, u32[]{:S(2)}) copy-start(bf16[8,64]{1,0:T(8,128)(2,1)} %rope_ref.1) | copy-start | bytes 3076

commit v5 on v4

--- a/solution.py
+++ b/solution.py
@@ -28,28 +28,35 @@
     return high, middle, (rest - middle).astype(BF16).astype(F32)
 
 
-def queries_kernel(queries_ref, latent_ref, gain_ref, sent_ref):
+def queries_kernel(nope, queries_ref, latent_ref, gain_ref, sent_hbm, tile_ref, sems):
     by_head = jnp.swapaxes(queries_ref[...].astype(F32), 0, 1)
     rows = by_head.reshape(64, by_head.shape[2])
+    rotated = jnp.concatenate([rows[:32, nope:], rows[32:, nope:]], 1)
     gain = jnp.concatenate([gain_ref[...].astype(F32), jnp.zeros((7, 32), F32)], 0)
-    extra = jnp.concatenate([latent_ref[...].astype(F32), gain], 1)
-    extra = jnp.concatenate([extra, jnp.zeros((56, 64), F32)], 0)
-    rows = jnp.concatenate([rows, extra], 1).astype(BF16)
-    for chip in range(CHIPS):
-        sent_ref[chip] = rows
-
-
-def own_kernel(width, q_ref, wuk_ref, full_ref):
-    nope = wuk_ref.shape[1]
+    extra = jnp.concatenate([latent_ref[...].astype(F32), gain, jnp.zeros((8, 64), F32)], 1)
+    extra = jnp.concatenate([extra, jnp.zeros((8, 128), F32)], 0)
+    tile_ref[...] = jnp.concatenate([rows[:, :nope], rotated, extra], 0).astype(BF16)
+    copies = [
+        pltpu.make_async_copy(tile_ref, sent_hbm.at[chip], sems.at[chip]) for chip in range(CHIPS)
+    ]
+    for copy in copies:
+        copy.start()
+    for copy in copies:
+        copy.wait()
+
+
+def own_kernel(q_ref, wuk_ref, full_ref):
     q = q_ref[0]
     parts = []
     for pair in range(4):
-        two = q[16 * pair : 16 * pair + 16, :nope]
+        two = q[16 * pair : 16 * pair + 16]
         first = jnp.dot(two, wuk_ref[2 * pair], preferred_element_type=F32)
         second = jnp.dot(two, wuk_ref[2 * pair + 1], preferred_element_type=F32)
         parts += [first[:8], second[8:]]
     absorbed = jnp.concatenate(parts, 0)
-    full_ref[...] = jnp.concatenate([absorbed, q[:, nope:width].astype(F32)], -1).astype(BF16)
+    rotated = q[64:96].astype(F32)
+    rotated = jnp.concatenate([rotated[:, :64], rotated[:, 64:]], 0)
+    full_ref[...] = jnp.concatenate([absorbed, rotated], -1).astype(BF16)
 
 
 def main_kernel(
@@ -84,17 +91,19 @@
     ]
     for copy in copies:
         copy.start()
-    nope, latent = wuk_ref.shape[1:]
+    latent = wuk_ref.shape[2]
 
     def absorb(pair):
         both = q_ref[:, 16 * pair : 16 * pair + 16, :].astype(F32).reshape(CHIPS, 2, 8, -1)
+        top, side = 64 + 16 * (pair % 2), 64 * (pair // 2)
+        rotated = q_ref[:, top : top + 16, :].astype(F32)[:, :, side : side + 64]
+        rotated = rotated.reshape(CHIPS, 2, 8, -1)
         fulls = []
         for j in range(2):
             one = both[:, j].reshape(128, -1).astype(BF16)
-            absorbed = jnp.dot(
-                one[:, :nope], wuk_ref[2 * pair + j], preferred_element_type=F32
-            ).astype(BF16)
-            fulls.append(jnp.concatenate([absorbed, one[:, nope:width]], -1))
+            absorbed = jnp.dot(one, wuk_ref[2 * pair + j], preferred_element_type=F32)
+            last = rotated[:, j].reshape(128, -1)
+            fulls.append(jnp.concatenate([absorbed, last], -1).astype(BF16))
         return fulls
 
     copies[0].wait()
@@ -153,8 +162,7 @@
 
 
 def attach_kernel(values_ref, stats_ref, moved_ref, out_ref):
-    moved = moved_ref[...].astype(F32)[:, :8, :].reshape(128, 128)
-    moved = pltpu.roll(moved, 64, 1).reshape(CHIPS, 8, 128)
+    moved = moved_ref[...].astype(F32)[:, :8, :]
     out_ref[:, :64, :] = values_ref[...]
     out_ref[:, 64:80, :] = jnp.concatenate([stats_ref[...], moved], 1).astype(BF16)
 
@@ -278,14 +286,19 @@
 ):
     width = queries.shape[2]
     scale = float(width) ** (-0.5)
-    sent = call(
-        queries_kernel, jax.ShapeDtypeStruct((CHIPS, 64, 256), BF16), 3, mib=62
+    sent = pl.pallas_call(
+        functools.partial(queries_kernel, w_uk.shape[1]),
+        out_shape=jax.ShapeDtypeStruct((CHIPS, 112, 128), BF16),
+        in_specs=[pl.BlockSpec(memory_space=VMEM)] * 3,
+        out_specs=pl.BlockSpec(memory_space=pl.ANY),
+        scratch_shapes=[VMEM((112, 128), BF16), pltpu.SemaphoreType.DMA((CHIPS,))],
+        compiler_params=pltpu.CompilerParams(vmem_limit_bytes=62 * 1024 * 1024),
     )(queries, new_latent, latent_gain[None])
     gathered = lax.all_to_all(sent, PLANE, 0, 0, axis_index_groups=[ORDER], tiled=True)
     keys = prompt_cache.T
     other = lax.ppermute(keys, "core", [(0, 1), (1, 0)])
     full = call(
-        functools.partial(own_kernel, width),
+        own_kernel,
         jax.ShapeDtypeStruct((64, keys.shape[0]), BF16),
         2,
         cost=30,
@@ -297,7 +310,7 @@
         for core in range(2)
         for z in range(16)
     ]
-    moved = lax.ppermute(gathered[:, :16, 128:], ("y", "x", "core", "z"), moves)
+    moved = lax.ppermute(gathered[:, 96:, :], ("y", "x", "core", "z"), moves)
 
     values, stats = call(
         functools.partial(main_kernel, width),

time: 55.9 us -> 55.6 us (level)
  no operation moved by 1% of the time
where the time goes in v5:
time: 55.6 us; the launch traced here: 54.8 us
  starting transfers between devices  31.5 us (57%)
  Pallas kernels  14.2 us (26%)
  waiting for transfers between devices  7.88 us (14%)
  local copies, waits for them, and re-layouts  1.05 us (2%)
    all_to_all x1, starting transfers between devices, per_device(): lax.all_to_all(parts, PLANE, 0, 0, axis_index_groups=[ORDER], tiled=True)  12.3 us
    all_to_all x1, starting transfers between devices, per_device(): lax.all_to_all(sent, PLANE, 0, 0, axis_index_groups=[ORDER], tiled=True)  10.4 us
    pallas_call x1, Pallas kernels, per_device(): call(functools.partial(main_kernel, width), (jax.ShapeDtypeStruct((CHIPS,...  8.63 us
    ppermute x1, starting transfers between devices, per_device(): moved = lax.ppermute(gathered[:, 96:, :], ('y', 'x', 'core', 'z'), moves)  6.88 us
    all_to_all x1, waiting for transfers between devices, per_device(): lax.all_to_all(parts, PLANE, 0, 0, axis_index_groups=[ORDER], tiled=True)  4.46 us
    all_to_all x1, waiting for transfers between devices, per_device(): lax.all_to_all(sent, PLANE, 0, 0, axis_index_groups=[ORDER], tiled=True)  3.41 us
    ppermute x1, starting transfers between devices, per_device(): other = lax.ppermute(keys, 'core', [(0, 1), (1, 0)])  1.91 us
    pallas_call x1, Pallas kernels, per_device(): pl.pallas_call(functools.partial(queries_kernel, w_uk.shape[1]), out_shap...  1.88 us
  transfers between devices with their start and end apart: 4, of which 2 were waited for; matrix products, arithmetic and copies ran while one was open for 0% of the time, Pallas kernels for 18%

profile of v5, /device:TPU:6, one launch (start us, length us, event | category | flops | bytes accessed | tf_op | source)
XLA Modules:
  0.0 54.8 jit_solution(15593147789408600253)
XLA Ops:
  0.0 0.0 copy-start.1
  0.0 1.9 %shard_map.91.q_ref = bf16[16,112,128]{2,1,0:T(8,128)(2,1)} custom-call(bf16[8,8,192]{2,1,0:T(8,128)(2,1)} %queries_ref.1, bf16[8,32]{1,0:T(8,128)(2,1)} %latent_ref.1, bf16[1,32]{1,0:T(2,128)(2,1)} %bitcast.4), custom_call_target="tpu_custom_call" | custom-call | tf_op jit(solution)/shard_map/pallas_call | solution.py:289
  1.9 10.4 %all-to-all-start = ((bf16[16,112,128]{2,1,0:T(8,128)(2,1)}), bf16[16,112,128]{2,1,0:T(8,128)(2,1)S(1)}, u32[]{:S(2)}, u32[]{:S(2)}) async-start(bf16[16,112,128]{2,1,0:T(8,128)(2,1)} %shard_map.91.q_ref), calls=%async_computation | async-start | bytes 917504 | tf_op jit(solution)/shard_map/all_to_all | solution.py:297
  12.3 1.9 %collective-permute-start = (bf16[576,1024]{1,0:T(8,128)(2,1)}, bf16[576,1024]{1,0:T(8,128)(2,1)}, u32[]{:S(2)}, u32[]{:S(2)}) collective-permute-start(bf16[576,1024]{1,0:T(8,128)(2,1)} %bitcast.5), channel_id=1, source_target_pairs={{0,16},{16,0},{1,17},{17,1},{2,18},{18,2},{3,19},{19,3},{4,20},{20... | collective-permute-start | bytes 3538952 | tf_op jit(solution)/shard_map/ppermute | solution.py:299
  14.2 0.0 copy-done.1
  14.2 0.0 copy-start
  14.2 1.0 %copy-done = bf16[16,112,128]{2,1,0:T(8,128)(2,1)S(1)} copy-done((bf16[16,112,128]{2,1,0:T(8,128)(2,1)S(1)}, bf16[16,112,128]{2,1,0:T(8,128)(2,1)}, u32[]{:S(2)}) %copy-start) | copy-done | bytes 458776
  15.3 0.2 shard_map.94.full_ref
  15.5 3.4 %all-to-all-done.q_hbm = bf16[16,112,128]{2,1,0:T(8,128)(2,1)S(1)} async-done(((bf16[16,112,128]{2,1,0:T(8,128)(2,1)}), bf16[16,112,128]{2,1,0:T(8,128)(2,1)S(1)}, u32[]{:S(2)}, u32[]{:S(2)}) %all-to-all-start) | async-done | bytes 458784 | tf_op jit(solution)/shard_map/all_to_all | solution.py:297
  18.9 6.9 %collective-permute-start.1 = (bf16[16,16,128]{2,1,0:T(8,128)(2,1)S(1)}, bf16[16,16,128]{2,1,0:T(8,128)(2,1)S(1)}, u32[]{:S(2)}, u32[]{:S(2)}) collective-permute-start(bf16[16,16,128]{2,1,0:T(8,128)(2,1)S(1)} %slice.4), channel_id=1, source_target_pairs={{320,328},{321,329},{322,330},{323,331},{324,332},{325,333},{326,3... | collective-permute-start | bytes 196616 | tf_op jit(solution)/shard_map/ppermute | solution.py:313
  25.8 0.0 collective-permute-done.kb_hbm
  25.8 8.6 %shard_map.92 = (bf16[16,64,128]{2,1,0:T(8,128)(2,1)S(1)}, f32[16,8,128]{2,1,0:T(8,128)S(1)}) custom-call(bf16[16,112,128]{2,1,0:T(8,128)(2,1)S(1)} %all-to-all-done.q_hbm, bf16[576,1024]{1,0:T(8,128)(2,1)} %bitcast.6, bf16[576,1024]{1,0:T(8,128)(2,1)} %collective-permute-done.kb_hbm, bf16[8,128,512]{2,1,0:T(8,128)(2,1)S(1)} %copy-done.1, ...), custom_call_target="tpu_custom_call" | custom-call | flops 8000000000 | tf_op jit(solution)/shard_map/pallas_call | solution.py:315
  34.4 0.0 collective-permute-done.1.moved_ref
  34.4 0.0 copy-start.2
  34.4 0.0 copy-start.3
  34.5 0.0 copy-start.5
  34.5 0.7 %shard_map.93 = bf16[16,80,128]{2,1,0:T(8,128)(2,1)} custom-call(bf16[16,64,128]{2,1,0:T(8,128)(2,1)S(1)} %get-tuple-element.9.values_ref, f32[16,8,128]{2,1,0:T(8,128)S(1)} %get-tuple-element.10.stats_ref, bf16[16,16,128]{2,1,0:T(8,128)(2,1)S(1)} %collective-permute-done.1.moved_ref), custom_call_target="tpu_custom_call" | custom-call | flops 1000000000 | tf_op jit(solution)/shard_map/pallas_call | solution.py:334
  35.2 12.3 %all-to-all-start.1 = ((bf16[16,80,128]{2,1,0:T(8,128)(2,1)}), bf16[16,80,128]{2,1,0:T(8,128)(2,1)S(1)}, u32[]{:S(2)}, u32[]{:S(2)}) async-start(bf16[16,80,128]{2,1,0:T(8,128)(2,1)} %shard_map.93), calls=%async_computation.1 | async-start | bytes 655360 | tf_op jit(solution)/shard_map/all_to_all | solution.py:337
  47.5 0.0 copy-done.2
  47.5 0.0 copy-done.3
  47.5 0.0 copy-done.5
  47.5 0.0 copy-start.4
  47.6 1.3 %shard_map.95 = (f32[64,128]{1,0:T(8,128)S(1)}, f32[16,128]{1,0:T(8,128)S(1)}) custom-call(bf16[64,576]{1,0:T(8,128)(2,1)S(1)} %shard_map.94.full_ref, bf16[2,576,256]{2,1,0:T(8,128)(2,1)S(1)} %bitcast.3, s32[2]{0:T(128)S(1)} %copy-done.5, bf16[8,512,128]{2,1,0:T(8,128)(2,1)S(1)} %copy-done.2), custom_call_target="tpu_custom_call" | custom-call | flops 5000000000 | tf_op jit(solution)/shard_map/pallas_call | solution.py:338
  48.8 4.5 %all-to-all-done.1.got_ref = bf16[16,80,128]{2,1,0:T(8,128)(2,1)S(1)} async-done(((bf16[16,80,128]{2,1,0:T(8,128)(2,1)}), bf16[16,80,128]{2,1,0:T(8,128)(2,1)S(1)}, u32[]{:S(2)}, u32[]{:S(2)}) %all-to-all-start.1) | async-done | bytes 327712 | tf_op jit(solution)/shard_map/all_to_all | solution.py:337
  53.3 0.0 copy-done.4
  53.3 1.5 %shard_map.96 = bf16[8,1024]{1,0:T(8,128)(2,1)} custom-call(bf16[16,80,128]{2,1,0:T(8,128)(2,1)S(1)} %all-to-all-done.1.got_ref, f32[64,128]{1,0:T(8,128)S(1)} %get-tuple-element.11.suffix_ref, f32[16,128]{1,0:T(8,128)S(1)} %get-tuple-element.12.suffix_stats_ref, bf16[64,576]{1,0:T(8,128)(2,1)S(1)} %shard_map.94.full_ref, bf16[8,64]{1,0:T(8,128)(2,1)S(1)} %copy-done.4, ...), custom_call_target="tpu_custom_call" | custom-call | flops 1000000000 | tf_op jit(solution)/shard_map/pallas_call | solution.py:345
  (1 shorter events, 0.0 us)
Async XLA Ops:
  0.0 14.2 %copy-start.1 = (bf16[8,128,512]{2,1,0:T(8,128)(2,1)S(1)}, bf16[8,128,512]{2,1,0:T(8,128)(2,1)}, u32[]{:S(2)}) copy-start(bf16[8,128,512]{2,1,0:T(8,128)(2,1)} %wuk_ref.1) | copy-start | bytes 3145732
  1.9 17.0 %all-to-all-start = ((bf16[16,112,128]{2,1,0:T(8,128)(2,1)}), bf16[16,112,128]{2,1,0:T(8,128)(2,1)S(1)}, u32[]{:S(2)}, u32[]{:S(2)}) async-start(bf16[16,112,128]{2,1,0:T(8,128)(2,1)} %shard_map.91.q_ref), calls=%async_computation | async-start | bytes 917504 | tf_op jit(solution)/shard_map/all_to_all | solution.py:297
  12.3 13.5 %collective-permute-start = (bf16[576,1024]{1,0:T(8,128)(2,1)}, bf16[576,1024]{1,0:T(8,128)(2,1)}, u32[]{:S(2)}, u32[]{:S(2)}) collective-permute-start(bf16[576,1024]{1,0:T(8,128)(2,1)} %bitcast.5), channel_id=1, source_target_pairs={{0,16},{16,0},{1,17},{17,1},{2,18},{18,2},{3,19},{19,3},{4,20},{20... | collective-permute-start | bytes 3538952 | tf_op jit(solution)/shard_map/ppermute | solution.py:299
  14.2 1.0 %copy-start = (bf16[16,112,128]{2,1,0:T(8,128)(2,1)S(1)}, bf16[16,112,128]{2,1,0:T(8,128)(2,1)}, u32[]{:S(2)}) copy-start(bf16[16,112,128]{2,1,0:T(8,128)(2,1)} %shard_map.91.q_ref) | copy-start | bytes 1376260
  18.9 15.5 %collective-permute-start.1 = (bf16[16,16,128]{2,1,0:T(8,128)(2,1)S(1)}, bf16[16,16,128]{2,1,0:T(8,128)(2,1)S(1)}, u32[]{:S(2)}, u32[]{:S(2)}) collective-permute-start(bf16[16,16,128]{2,1,0:T(8,128)(2,1)S(1)} %slice.4), channel_id=1, source_target_pairs={{320,328},{321,329},{322,330},{323,331},{324,332},{325,333},{326,3... | collective-permute-start | bytes 196616 | tf_op jit(solution)/shard_map/ppermute | solution.py:313
  34.4 13.1 %copy-start.2 = (bf16[8,512,128]{2,1,0:T(8,128)(2,1)S(1)}, bf16[8,512,128]{2,1,0:T(8,128)(2,1)}, u32[]{:S(2)}) copy-start(bf16[8,512,128]{2,1,0:T(8,128)(2,1)} %wuv_ref.3) | copy-start | bytes 3145732
  34.4 13.1 %copy-start.3 = (bf16[2,256,576]{1,2,0:T(8,128)(2,1)S(1)}, bf16[2,256,576]{1,2,0:T(8,128)(2,1)}, u32[]{:S(2)}) copy-start(bf16[2,256,576]{1,2,0:T(8,128)(2,1)} %param.11) | copy-start | bytes 1769476
  34.5 13.1 %copy-start.5 = (s32[2]{0:T(128)S(1)}, s32[2]{0:T(128)}, u32[]{:S(2)}) copy-start(s32[2]{0:T(128)} %lengths_ref.1) | copy-start | bytes 28
  35.2 18.1 %all-to-all-start.1 = ((bf16[16,80,128]{2,1,0:T(8,128)(2,1)}), bf16[16,80,128]{2,1,0:T(8,128)(2,1)S(1)}, u32[]{:S(2)}, u32[]{:S(2)}) async-start(bf16[16,80,128]{2,1,0:T(8,128)(2,1)} %shard_map.93), calls=%async_computation.1 | async-start | bytes 655360 | tf_op jit(solution)/shard_map/all_to_all | solution.py:337
  47.5 5.8 %copy-start.4 = (bf16[8,64]{1,0:T(8,128)(2,1)S(1)}, bf16[8,64]{1,0:T(8,128)(2,1)}, u32[]{:S(2)}) copy-start(bf16[8,64]{1,0:T(8,128)(2,1)} %rope_ref.1) | copy-start | bytes 3076

commit v6 on v5

--- a/solution.py
+++ b/solution.py
@@ -61,17 +61,15 @@
 
 def main_kernel(
     width,
-    q_hbm,
+    q_ref,
     ka_hbm,
     kb_hbm,
-    wuk_hbm,
+    wuk_ref,
     wuv_hbm,
     out_ref,
     stats_ref,
-    q_ref,
     ka_ref,
     kb_ref,
-    wuk_ref,
     wuv_ref,
     sems,
 ):
@@ -80,17 +78,13 @@
         pltpu.make_async_copy(source, target, sems.at[i])
         for i, (source, target) in enumerate(
             [
-                (q_hbm, q_ref),
-                (wuk_hbm.at[:2], wuk_ref.at[:2]),
                 (ka_hbm, ka_ref),
-                (wuk_hbm.at[2:], wuk_ref.at[2:]),
                 (kb_hbm, kb_ref),
                 (wuv_hbm, wuv_ref),
             ]
         )
     ]
-    for copy in copies:
-        copy.start()
+    copies[0].start()
     latent = wuk_ref.shape[2]
 
     def absorb(pair):
@@ -106,13 +100,12 @@
             fulls.append(jnp.concatenate([absorbed, last], -1).astype(BF16))
         return fulls
 
+    fulls = []
+    for pair in range(4):
+        fulls += absorb(pair)
     copies[0].wait()
-    copies[1].wait()
-    fulls = absorb(0)
-    copies[2].wait()
-    copies[3].wait()
-    for pair in range(1, 4):
-        fulls += absorb(pair)
+    copies[1].start()
+    copies[2].start()
     full = jnp.concatenate(fulls, 0)
 
     half = ka_ref.shape[1] // 2
@@ -124,9 +117,9 @@
     scores = score(*blocks[0])
     peak = None
     for i, (keys, at) in enumerate(blocks):
-        if i == 0:
-            copies[4].wait()
-            copies[5].wait()
+        if i == 1:
+            copies[1].wait()
+            copies[2].wait()
         later = score(*blocks[i + 1]) if i < 3 else None
         top = jnp.max(scores, -1, keepdims=True)
         top = top if peak is None else jnp.maximum(peak, top)
@@ -319,14 +312,12 @@
             jax.ShapeDtypeStruct((CHIPS, 8, 128), F32),
         ),
         5,
-        hbm=(0, 1, 2, 3, 4),
+        hbm=(1, 2, 4),
         scratch=[
-            VMEM(gathered.shape, BF16),
             VMEM(keys.shape, BF16),
             VMEM(keys.shape, BF16),
-            VMEM(w_uk.shape, BF16),
             VMEM(w_uv.shape, BF16),
-            pltpu.SemaphoreType.DMA((6,)),
+            pltpu.SemaphoreType.DMA((3,)),
         ],
         cost=8,
         mib=52,

time: 55.6 us -> 55.5 us (level)
  no operation moved by 1% of the time
where the time goes in v6:
time: 55.5 us; the launch traced here: 54.7 us
  starting transfers between devices  31.5 us (57%)
  Pallas kernels  14.1 us (25%)
  waiting for transfers between devices  7.88 us (14%)
  local copies, waits for them, and re-layouts  1.05 us (2%)
    all_to_all x1, starting transfers between devices, per_device(): lax.all_to_all(parts, PLANE, 0, 0, axis_index_groups=[ORDER], tiled=True)  12.3 us
    all_to_all x1, starting transfers between devices, per_device(): lax.all_to_all(sent, PLANE, 0, 0, axis_index_groups=[ORDER], tiled=True)  10.4 us
    pallas_call x1, Pallas kernels, per_device(): call(functools.partial(main_kernel, width), (jax.ShapeDtypeStruct((CHIPS,...  8.53 us
    ppermute x1, starting transfers between devices, per_device(): moved = lax.ppermute(gathered[:, 96:, :], ('y', 'x', 'core', 'z'), moves)  6.88 us
    all_to_all x1, waiting for transfers between devices, per_device(): lax.all_to_all(parts, PLANE, 0, 0, axis_index_groups=[ORDER], tiled=True)  4.46 us
    all_to_all x1, waiting for transfers between devices, per_device(): lax.all_to_all(sent, PLANE, 0, 0, axis_index_groups=[ORDER], tiled=True)  3.41 us
    ppermute x1, starting transfers between devices, per_device(): other = lax.ppermute(keys, 'core', [(0, 1), (1, 0)])  1.91 us
    pallas_call x1, Pallas kernels, per_device(): pl.pallas_call(functools.partial(queries_kernel, w_uk.shape[1]), out_shap...  1.88 us
  transfers between devices with their start and end apart: 4, of which 2 were waited for; matrix products, arithmetic and copies ran while one was open for 0% of the time, Pallas kernels for 18%

profile of v6, /device:TPU:6, one launch (start us, length us, event | category | flops | bytes accessed | tf_op | source)
XLA Modules:
  0.0 54.7 jit_solution(895227863942837206)
XLA Ops:
  0.0 0.0 copy-start.1
  0.0 1.9 %shard_map.91.q_ref = bf16[16,112,128]{2,1,0:T(8,128)(2,1)} custom-call(bf16[8,8,192]{2,1,0:T(8,128)(2,1)} %queries_ref.1, bf16[8,32]{1,0:T(8,128)(2,1)} %latent_ref.1, bf16[1,32]{1,0:T(2,128)(2,1)} %bitcast.4), custom_call_target="tpu_custom_call" | custom-call | tf_op jit(solution)/shard_map/pallas_call | solution.py:282
  1.9 10.4 %all-to-all-start = ((bf16[16,112,128]{2,1,0:T(8,128)(2,1)}), bf16[16,112,128]{2,1,0:T(8,128)(2,1)S(1)}, u32[]{:S(2)}, u32[]{:S(2)}) async-start(bf16[16,112,128]{2,1,0:T(8,128)(2,1)} %shard_map.91.q_ref), calls=%async_computation | async-start | bytes 917504 | tf_op jit(solution)/shard_map/all_to_all | solution.py:290
  12.3 1.9 %collective-permute-start = (bf16[576,1024]{1,0:T(8,128)(2,1)}, bf16[576,1024]{1,0:T(8,128)(2,1)}, u32[]{:S(2)}, u32[]{:S(2)}) collective-permute-start(bf16[576,1024]{1,0:T(8,128)(2,1)} %bitcast.5), channel_id=1, source_target_pairs={{0,16},{16,0},{1,17},{17,1},{2,18},{18,2},{3,19},{19,3},{4,20},{20... | collective-permute-start | bytes 3538952 | tf_op jit(solution)/shard_map/ppermute | solution.py:292
  14.2 0.0 copy-done.1
  14.2 0.0 copy-start
  14.2 1.0 %copy-done = bf16[16,112,128]{2,1,0:T(8,128)(2,1)S(1)} copy-done((bf16[16,112,128]{2,1,0:T(8,128)(2,1)S(1)}, bf16[16,112,128]{2,1,0:T(8,128)(2,1)}, u32[]{:S(2)}) %copy-start) | copy-done | bytes 458776
  15.3 0.2 shard_map.94.full_ref
  15.5 3.4 %all-to-all-done.q_ref = bf16[16,112,128]{2,1,0:T(8,128)(2,1)S(1)} async-done(((bf16[16,112,128]{2,1,0:T(8,128)(2,1)}), bf16[16,112,128]{2,1,0:T(8,128)(2,1)S(1)}, u32[]{:S(2)}, u32[]{:S(2)}) %all-to-all-start) | async-done | bytes 458784 | tf_op jit(solution)/shard_map/all_to_all | solution.py:290
  18.9 6.9 %collective-permute-start.1 = (bf16[16,16,128]{2,1,0:T(8,128)(2,1)S(1)}, bf16[16,16,128]{2,1,0:T(8,128)(2,1)S(1)}, u32[]{:S(2)}, u32[]{:S(2)}) collective-permute-start(bf16[16,16,128]{2,1,0:T(8,128)(2,1)S(1)} %slice.4), channel_id=1, source_target_pairs={{320,328},{321,329},{322,330},{323,331},{324,332},{325,333},{326,3... | collective-permute-start | bytes 196616 | tf_op jit(solution)/shard_map/ppermute | solution.py:306
  25.8 0.0 collective-permute-done.kb_hbm
  25.8 8.5 %shard_map.92 = (bf16[16,64,128]{2,1,0:T(8,128)(2,1)S(1)}, f32[16,8,128]{2,1,0:T(8,128)S(1)}) custom-call(bf16[16,112,128]{2,1,0:T(8,128)(2,1)S(1)} %all-to-all-done.q_ref, bf16[576,1024]{1,0:T(8,128)(2,1)} %bitcast.6, bf16[576,1024]{1,0:T(8,128)(2,1)} %collective-permute-done.kb_hbm, bf16[8,128,512]{2,1,0:T(8,128)(2,1)S(1)} %copy-done.1, ...), custom_call_target="tpu_custom_call" | custom-call | flops 8000000000 | tf_op jit(solution)/shard_map/pallas_call | solution.py:308
  34.3 0.0 collective-permute-done.1.moved_ref
  34.3 0.0 copy-start.2
  34.3 0.0 copy-start.3
  34.4 0.0 copy-start.5
  34.4 0.7 %shard_map.93 = bf16[16,80,128]{2,1,0:T(8,128)(2,1)} custom-call(bf16[16,64,128]{2,1,0:T(8,128)(2,1)S(1)} %get-tuple-element.9.values_ref, f32[16,8,128]{2,1,0:T(8,128)S(1)} %get-tuple-element.10.stats_ref, bf16[16,16,128]{2,1,0:T(8,128)(2,1)S(1)} %collective-permute-done.1.moved_ref), custom_call_target="tpu_custom_call" | custom-call | flops 1000000000 | tf_op jit(solution)/shard_map/pallas_call | solution.py:325
  35.1 12.3 %all-to-all-start.1 = ((bf16[16,80,128]{2,1,0:T(8,128)(2,1)}), bf16[16,80,128]{2,1,0:T(8,128)(2,1)S(1)}, u32[]{:S(2)}, u32[]{:S(2)}) async-start(bf16[16,80,128]{2,1,0:T(8,128)(2,1)} %shard_map.93), calls=%async_computation.1 | async-start | bytes 655360 | tf_op jit(solution)/shard_map/all_to_all | solution.py:328
  47.4 0.0 copy-done.2
  47.4 0.0 copy-done.3
  47.4 0.0 copy-done.5
  47.4 0.0 copy-start.4
  47.4 1.3 %shard_map.95 = (f32[64,128]{1,0:T(8,128)S(1)}, f32[16,128]{1,0:T(8,128)S(1)}) custom-call(bf16[64,576]{1,0:T(8,128)(2,1)S(1)} %shard_map.94.full_ref, bf16[2,576,256]{2,1,0:T(8,128)(2,1)S(1)} %bitcast.3, s32[2]{0:T(128)S(1)} %copy-done.5, bf16[8,512,128]{2,1,0:T(8,128)(2,1)S(1)} %copy-done.2), custom_call_target="tpu_custom_call" | custom-call | flops 5000000000 | tf_op jit(solution)/shard_map/pallas_call | solution.py:329
  48.7 4.5 %all-to-all-done.1.got_ref = bf16[16,80,128]{2,1,0:T(8,128)(2,1)S(1)} async-done(((bf16[16,80,128]{2,1,0:T(8,128)(2,1)}), bf16[16,80,128]{2,1,0:T(8,128)(2,1)S(1)}, u32[]{:S(2)}, u32[]{:S(2)}) %all-to-all-start.1) | async-done | bytes 327712 | tf_op jit(solution)/shard_map/all_to_all | solution.py:328
  53.2 0.0 copy-done.4
  53.2 1.5 %shard_map.96 = bf16[8,1024]{1,0:T(8,128)(2,1)} custom-call(bf16[16,80,128]{2,1,0:T(8,128)(2,1)S(1)} %all-to-all-done.1.got_ref, f32[64,128]{1,0:T(8,128)S(1)} %get-tuple-element.11.suffix_ref, f32[16,128]{1,0:T(8,128)S(1)} %get-tuple-element.12.suffix_stats_ref, bf16[64,576]{1,0:T(8,128)(2,1)S(1)} %shard_map.94.full_ref, bf16[8,64]{1,0:T(8,128)(2,1)S(1)} %copy-done.4, ...), custom_call_target="tpu_custom_call" | custom-call | flops 1000000000 | tf_op jit(solution)/shard_map/pallas_call | solution.py:336
  (1 shorter events, 0.0 us)
Async XLA Ops:
  0.0 14.2 %copy-start.1 = (bf16[8,128,512]{2,1,0:T(8,128)(2,1)S(1)}, bf16[8,128,512]{2,1,0:T(8,128)(2,1)}, u32[]{:S(2)}) copy-start(bf16[8,128,512]{2,1,0:T(8,128)(2,1)} %wuk_ref.3) | copy-start | bytes 3145732
  1.9 17.0 %all-to-all-start = ((bf16[16,112,128]{2,1,0:T(8,128)(2,1)}), bf16[16,112,128]{2,1,0:T(8,128)(2,1)S(1)}, u32[]{:S(2)}, u32[]{:S(2)}) async-start(bf16[16,112,128]{2,1,0:T(8,128)(2,1)} %shard_map.91.q_ref), calls=%async_computation | async-start | bytes 917504 | tf_op jit(solution)/shard_map/all_to_all | solution.py:290
  12.3 13.5 %collective-permute-start = (bf16[576,1024]{1,0:T(8,128)(2,1)}, bf16[576,1024]{1,0:T(8,128)(2,1)}, u32[]{:S(2)}, u32[]{:S(2)}) collective-permute-start(bf16[576,1024]{1,0:T(8,128)(2,1)} %bitcast.5), channel_id=1, source_target_pairs={{0,16},{16,0},{1,17},{17,1},{2,18},{18,2},{3,19},{19,3},{4,20},{20... | collective-permute-start | bytes 3538952 | tf_op jit(solution)/shard_map/ppermute | solution.py:292
  14.2 1.0 %copy-start = (bf16[16,112,128]{2,1,0:T(8,128)(2,1)S(1)}, bf16[16,112,128]{2,1,0:T(8,128)(2,1)}, u32[]{:S(2)}) copy-start(bf16[16,112,128]{2,1,0:T(8,128)(2,1)} %shard_map.91.q_ref) | copy-start | bytes 1376260
  18.9 15.4 %collective-permute-start.1 = (bf16[16,16,128]{2,1,0:T(8,128)(2,1)S(1)}, bf16[16,16,128]{2,1,0:T(8,128)(2,1)S(1)}, u32[]{:S(2)}, u32[]{:S(2)}) collective-permute-start(bf16[16,16,128]{2,1,0:T(8,128)(2,1)S(1)} %slice.4), channel_id=1, source_target_pairs={{320,328},{321,329},{322,330},{323,331},{324,332},{325,333},{326,3... | collective-permute-start | bytes 196616 | tf_op jit(solution)/shard_map/ppermute | solution.py:306
  34.3 13.1 %copy-start.2 = (bf16[8,512,128]{2,1,0:T(8,128)(2,1)S(1)}, bf16[8,512,128]{2,1,0:T(8,128)(2,1)}, u32[]{:S(2)}) copy-start(bf16[8,512,128]{2,1,0:T(8,128)(2,1)} %wuv_ref.3) | copy-start | bytes 3145732
  34.3 13.1 %copy-start.3 = (bf16[2,256,576]{1,2,0:T(8,128)(2,1)S(1)}, bf16[2,256,576]{1,2,0:T(8,128)(2,1)}, u32[]{:S(2)}) copy-start(bf16[2,256,576]{1,2,0:T(8,128)(2,1)} %param.11) | copy-start | bytes 1769476
  34.4 13.1 %copy-start.5 = (s32[2]{0:T(128)S(1)}, s32[2]{0:T(128)}, u32[]{:S(2)}) copy-start(s32[2]{0:T(128)} %lengths_ref.1) | copy-start | bytes 28
  35.1 18.1 %all-to-all-start.1 = ((bf16[16,80,128]{2,1,0:T(8,128)(2,1)}), bf16[16,80,128]{2,1,0:T(8,128)(2,1)S(1)}, u32[]{:S(2)}, u32[]{:S(2)}) async-start(bf16[16,80,128]{2,1,0:T(8,128)(2,1)} %shard_map.93), calls=%async_computation.1 | async-start | bytes 655360 | tf_op jit(solution)/shard_map/all_to_all | solution.py:328
  47.4 5.8 %copy-start.4 = (bf16[8,64]{1,0:T(8,128)(2,1)S(1)}, bf16[8,64]{1,0:T(8,128)(2,1)}, u32[]{:S(2)}) copy-start(bf16[8,64]{1,0:T(8,128)(2,1)} %rope_ref.1) | copy-start | bytes 3076

commit v7 on v6

--- a/solution.py
+++ b/solution.py
@@ -212,7 +212,8 @@
     for g in range(4):
         latent, gain = 0.0, 0.0
         for j in range(4):
-            chip = ((place - (4 * g + j)) & 15) ^ 8
+            away = ((place - (4 * g + j)) & 15) - 8
+            chip = jnp.minimum(jnp.where(away > 0, 2 * away - 1, -2 * away), 15)
             piece = got_ref[chip, 64:80, :].astype(F32)[8:]
             one = jnp.where(lane == 0, piece, 0.0)
             latent = latent + (pltpu.roll(one, 32 * j, 1) if j else one)
@@ -297,8 +298,11 @@
         cost=30,
     )(sent, w_uk)
 
+    def step(k):
+        return 8 + (k // 2 + 1 if k % 2 else -(k // 2))
+
     moves = [
-        ((2 * p + core) * 16 + z, (2 * p + core) * 16 + (z + (8 ^ k)) % 16)
+        ((2 * p + core) * 16 + z, (2 * p + core) * 16 + (z + step(k)) % 16)
         for k, p in enumerate(ORDER)
         for core in range(2)
         for z in range(16)

time: 55.5 us -> 55.5 us (level)
  waiting for transfers between devices: 7.88 us -> 8.76 us
  starting transfers between devices: 31.5 us -> 30.7 us
    ppermute x1, starting transfers between devices: 6.88 us -> 2.96 us  [per_device(): moved = lax.ppermute(gathered[:, 96:, :], ('y', 'x', 'core', 'z'), moves)]
    all_to_all x1, starting transfers between devices: 12.3 us -> 15.4 us  [per_device(): lax.all_to_all(parts, PLANE, 0, 0, axis_index_groups=[ORDER], tiled=True)]
    ppermute x1, waiting for transfers between devices: 0.01 us -> 0.89 us  [per_device(): moved = lax.ppermute(gathered[:, 96:, :], ('y', 'x', 'core', 'z'), moves)]
  transfers between devices with their start and end apart: 4 -> 4, of which waited for: 2 -> 3; matrix products, arithmetic and copies ran while one was open for 0% -> 0% of each run, Pallas kernels for 18% -> 18%
where the time goes in v7:
time: 55.5 us; the launch traced here: 54.7 us
  starting transfers between devices  30.7 us (55%)
  Pallas kernels  14.2 us (26%)
  waiting for transfers between devices  8.76 us (16%)
  local copies, waits for them, and re-layouts  1.04 us (2%)
    all_to_all x1, starting transfers between devices, per_device(): lax.all_to_all(parts, PLANE, 0, 0, axis_index_groups=[ORDER], tiled=True)  15.4 us
    all_to_all x1, starting transfers between devices, per_device(): lax.all_to_all(sent, PLANE, 0, 0, axis_index_groups=[ORDER], tiled=True)  10.4 us
    pallas_call x1, Pallas kernels, per_device(): call(functools.partial(main_kernel, width), (jax.ShapeDtypeStruct((CHIPS,...  8.54 us
    all_to_all x1, waiting for transfers between devices, per_device(): lax.all_to_all(parts, PLANE, 0, 0, axis_index_groups=[ORDER], tiled=True)  4.46 us
    all_to_all x1, waiting for transfers between devices, per_device(): lax.all_to_all(sent, PLANE, 0, 0, axis_index_groups=[ORDER], tiled=True)  3.41 us
    ppermute x1, starting transfers between devices, per_device(): moved = lax.ppermute(gathered[:, 96:, :], ('y', 'x', 'core', 'z'), moves)  2.96 us
    ppermute x1, starting transfers between devices, per_device(): other = lax.ppermute(keys, 'core', [(0, 1), (1, 0)])  1.91 us
    pallas_call x1, Pallas kernels, per_device(): pl.pallas_call(functools.partial(queries_kernel, w_uk.shape[1]), out_shap...  1.88 us
  transfers between devices with their start and end apart: 4, of which 3 were waited for; matrix products, arithmetic and copies ran while one was open for 0% of the time, Pallas kernels for 18%

profile of v7, /device:TPU:6, one launch (start us, length us, event | category | flops | bytes accessed | tf_op | source)
XLA Modules:
  0.0 54.7 jit_solution(3516626809002059112)
XLA Ops:
  0.0 0.0 copy-start.1
  0.0 1.9 %shard_map.91.q_ref = bf16[16,112,128]{2,1,0:T(8,128)(2,1)} custom-call(bf16[8,8,192]{2,1,0:T(8,128)(2,1)} %queries_ref.1, bf16[8,32]{1,0:T(8,128)(2,1)} %latent_ref.1, bf16[1,32]{1,0:T(2,128)(2,1)} %bitcast.4), custom_call_target="tpu_custom_call" | custom-call | tf_op jit(solution)/shard_map/pallas_call | solution.py:283
  1.9 10.4 %all-to-all-start = ((bf16[16,112,128]{2,1,0:T(8,128)(2,1)}), bf16[16,112,128]{2,1,0:T(8,128)(2,1)S(1)}, u32[]{:S(2)}, u32[]{:S(2)}) async-start(bf16[16,112,128]{2,1,0:T(8,128)(2,1)} %shard_map.91.q_ref), calls=%async_computation | async-start | bytes 917504 | tf_op jit(solution)/shard_map/all_to_all | solution.py:291
  12.3 1.9 %collective-permute-start = (bf16[576,1024]{1,0:T(8,128)(2,1)}, bf16[576,1024]{1,0:T(8,128)(2,1)}, u32[]{:S(2)}, u32[]{:S(2)}) collective-permute-start(bf16[576,1024]{1,0:T(8,128)(2,1)} %bitcast.5), channel_id=1, source_target_pairs={{0,16},{16,0},{1,17},{17,1},{2,18},{18,2},{3,19},{19,3},{4,20},{20... | collective-permute-start | bytes 3538952 | tf_op jit(solution)/shard_map/ppermute | solution.py:293
  14.2 0.0 copy-done.1
  14.2 0.0 copy-start
  14.2 1.0 %copy-done = bf16[16,112,128]{2,1,0:T(8,128)(2,1)S(1)} copy-done((bf16[16,112,128]{2,1,0:T(8,128)(2,1)S(1)}, bf16[16,112,128]{2,1,0:T(8,128)(2,1)}, u32[]{:S(2)}) %copy-start) | copy-done | bytes 458776
  15.3 0.2 shard_map.94.full_ref
  15.5 3.4 %all-to-all-done.q_ref = bf16[16,112,128]{2,1,0:T(8,128)(2,1)S(1)} async-done(((bf16[16,112,128]{2,1,0:T(8,128)(2,1)}), bf16[16,112,128]{2,1,0:T(8,128)(2,1)S(1)}, u32[]{:S(2)}, u32[]{:S(2)}) %all-to-all-start) | async-done | bytes 458784 | tf_op jit(solution)/shard_map/all_to_all | solution.py:291
  18.9 3.0 %collective-permute-start.1 = (bf16[16,16,128]{2,1,0:T(8,128)(2,1)S(1)}, bf16[16,16,128]{2,1,0:T(8,128)(2,1)S(1)}, u32[]{:S(2)}, u32[]{:S(2)}) collective-permute-start(bf16[16,16,128]{2,1,0:T(8,128)(2,1)S(1)} %slice.4), channel_id=1, source_target_pairs={{320,328},{321,329},{322,330},{323,331},{324,332},{325,333},{326,3... | collective-permute-start | bytes 196616 | tf_op jit(solution)/shard_map/ppermute | solution.py:310
  21.9 0.0 collective-permute-done.kb_hbm
  21.9 8.5 %shard_map.92 = (bf16[16,64,128]{2,1,0:T(8,128)(2,1)S(1)}, f32[16,8,128]{2,1,0:T(8,128)S(1)}) custom-call(bf16[16,112,128]{2,1,0:T(8,128)(2,1)S(1)} %all-to-all-done.q_ref, bf16[576,1024]{1,0:T(8,128)(2,1)} %bitcast.6, bf16[576,1024]{1,0:T(8,128)(2,1)} %collective-permute-done.kb_hbm, bf16[8,128,512]{2,1,0:T(8,128)(2,1)S(1)} %copy-done.1, ...), custom_call_target="tpu_custom_call" | custom-call | flops 8000000000 | tf_op jit(solution)/shard_map/pallas_call | solution.py:312
  30.4 0.9 %collective-permute-done.1.moved_ref = bf16[16,16,128]{2,1,0:T(8,128)(2,1)S(1)} collective-permute-done((bf16[16,16,128]{2,1,0:T(8,128)(2,1)S(1)}, bf16[16,16,128]{2,1,0:T(8,128)(2,1)S(1)}, u32[]{:S(2)}, u32[]{:S(2)}) %collective-permute-start.1) | collective-permute-done | bytes 65568 | tf_op jit(solution)/shard_map/ppermute | solution.py:310
  31.3 0.0 copy-start.2
  31.3 0.0 copy-start.3
  31.3 0.0 copy-start.5
  31.3 0.7 %shard_map.93 = bf16[16,80,128]{2,1,0:T(8,128)(2,1)} custom-call(bf16[16,64,128]{2,1,0:T(8,128)(2,1)S(1)} %get-tuple-element.9.values_ref, f32[16,8,128]{2,1,0:T(8,128)S(1)} %get-tuple-element.10.stats_ref, bf16[16,16,128]{2,1,0:T(8,128)(2,1)S(1)} %collective-permute-done.1.moved_ref), custom_call_target="tpu_custom_call" | custom-call | flops 1000000000 | tf_op jit(solution)/shard_map/pallas_call | solution.py:329
  32.0 15.4 %all-to-all-start.1 = ((bf16[16,80,128]{2,1,0:T(8,128)(2,1)}), bf16[16,80,128]{2,1,0:T(8,128)(2,1)S(1)}, u32[]{:S(2)}, u32[]{:S(2)}) async-start(bf16[16,80,128]{2,1,0:T(8,128)(2,1)} %shard_map.93), calls=%async_computation.1 | async-start | bytes 655360 | tf_op jit(solution)/shard_map/all_to_all | solution.py:332
  47.4 0.0 copy-done.2
  47.4 0.0 copy-done.3
  47.4 0.0 copy-done.5
  47.4 0.0 copy-start.4
  47.4 1.3 %shard_map.95 = (f32[64,128]{1,0:T(8,128)S(1)}, f32[16,128]{1,0:T(8,128)S(1)}) custom-call(bf16[64,576]{1,0:T(8,128)(2,1)S(1)} %shard_map.94.full_ref, bf16[2,576,256]{2,1,0:T(8,128)(2,1)S(1)} %bitcast.3, s32[2]{0:T(128)S(1)} %copy-done.5, bf16[8,512,128]{2,1,0:T(8,128)(2,1)S(1)} %copy-done.2), custom_call_target="tpu_custom_call" | custom-call | flops 5000000000 | tf_op jit(solution)/shard_map/pallas_call | solution.py:333
  48.7 4.5 %all-to-all-done.1.got_ref = bf16[16,80,128]{2,1,0:T(8,128)(2,1)S(1)} async-done(((bf16[16,80,128]{2,1,0:T(8,128)(2,1)}), bf16[16,80,128]{2,1,0:T(8,128)(2,1)S(1)}, u32[]{:S(2)}, u32[]{:S(2)}) %all-to-all-start.1) | async-done | bytes 327712 | tf_op jit(solution)/shard_map/all_to_all | solution.py:332
  53.2 0.0 copy-done.4
  53.2 1.5 %shard_map.96 = bf16[8,1024]{1,0:T(8,128)(2,1)} custom-call(bf16[16,80,128]{2,1,0:T(8,128)(2,1)S(1)} %all-to-all-done.1.got_ref, f32[64,128]{1,0:T(8,128)S(1)} %get-tuple-element.11.suffix_ref, f32[16,128]{1,0:T(8,128)S(1)} %get-tuple-element.12.suffix_stats_ref, bf16[64,576]{1,0:T(8,128)(2,1)S(1)} %shard_map.94.full_ref, bf16[8,64]{1,0:T(8,128)(2,1)S(1)} %copy-done.4, ...), custom_call_target="tpu_custom_call" | custom-call | flops 1000000000 | tf_op jit(solution)/shard_map/pallas_call | solution.py:340
  (1 shorter events, 0.0 us)
Async XLA Ops:
  0.0 14.2 %copy-start.1 = (bf16[8,128,512]{2,1,0:T(8,128)(2,1)S(1)}, bf16[8,128,512]{2,1,0:T(8,128)(2,1)}, u32[]{:S(2)}) copy-start(bf16[8,128,512]{2,1,0:T(8,128)(2,1)} %wuk_ref.3) | copy-start | bytes 3145732
  1.9 17.0 %all-to-all-start = ((bf16[16,112,128]{2,1,0:T(8,128)(2,1)}), bf16[16,112,128]{2,1,0:T(8,128)(2,1)S(1)}, u32[]{:S(2)}, u32[]{:S(2)}) async-start(bf16[16,112,128]{2,1,0:T(8,128)(2,1)} %shard_map.91.q_ref), calls=%async_computation | async-start | bytes 917504 | tf_op jit(solution)/shard_map/all_to_all | solution.py:291
  12.3 9.6 %collective-permute-start = (bf16[576,1024]{1,0:T(8,128)(2,1)}, bf16[576,1024]{1,0:T(8,128)(2,1)}, u32[]{:S(2)}, u32[]{:S(2)}) collective-permute-start(bf16[576,1024]{1,0:T(8,128)(2,1)} %bitcast.5), channel_id=1, source_target_pairs={{0,16},{16,0},{1,17},{17,1},{2,18},{18,2},{3,19},{19,3},{4,20},{20... | collective-permute-start | bytes 3538952 | tf_op jit(solution)/shard_map/ppermute | solution.py:293
  14.2 1.0 %copy-start = (bf16[16,112,128]{2,1,0:T(8,128)(2,1)S(1)}, bf16[16,112,128]{2,1,0:T(8,128)(2,1)}, u32[]{:S(2)}) copy-start(bf16[16,112,128]{2,1,0:T(8,128)(2,1)} %shard_map.91.q_ref) | copy-start | bytes 1376260
  18.9 12.4 %collective-permute-start.1 = (bf16[16,16,128]{2,1,0:T(8,128)(2,1)S(1)}, bf16[16,16,128]{2,1,0:T(8,128)(2,1)S(1)}, u32[]{:S(2)}, u32[]{:S(2)}) collective-permute-start(bf16[16,16,128]{2,1,0:T(8,128)(2,1)S(1)} %slice.4), channel_id=1, source_target_pairs={{320,328},{321,329},{322,330},{323,331},{324,332},{325,333},{326,3... | collective-permute-start | bytes 196616 | tf_op jit(solution)/shard_map/ppermute | solution.py:310
  31.3 16.1 %copy-start.2 = (bf16[8,512,128]{2,1,0:T(8,128)(2,1)S(1)}, bf16[8,512,128]{2,1,0:T(8,128)(2,1)}, u32[]{:S(2)}) copy-start(bf16[8,512,128]{2,1,0:T(8,128)(2,1)} %wuv_ref.3) | copy-start | bytes 3145732
  31.3 16.1 %copy-start.3 = (bf16[2,256,576]{1,2,0:T(8,128)(2,1)S(1)}, bf16[2,256,576]{1,2,0:T(8,128)(2,1)}, u32[]{:S(2)}) copy-start(bf16[2,256,576]{1,2,0:T(8,128)(2,1)} %param.11) | copy-start | bytes 1769476
  31.3 16.1 %copy-start.5 = (s32[2]{0:T(128)S(1)}, s32[2]{0:T(128)}, u32[]{:S(2)}) copy-start(s32[2]{0:T(128)} %lengths_ref.1) | copy-start | bytes 28
  32.0 21.1 %all-to-all-start.1 = ((bf16[16,80,128]{2,1,0:T(8,128)(2,1)}), bf16[16,80,128]{2,1,0:T(8,128)(2,1)S(1)}, u32[]{:S(2)}, u32[]{:S(2)}) async-start(bf16[16,80,128]{2,1,0:T(8,128)(2,1)} %shard_map.93), calls=%async_computation.1 | async-start | bytes 655360 | tf_op jit(solution)/shard_map/all_to_all | solution.py:332
  47.4 5.8 %copy-start.4 = (bf16[8,64]{1,0:T(8,128)(2,1)S(1)}, bf16[8,64]{1,0:T(8,128)(2,1)}, u32[]{:S(2)}) copy-start(bf16[8,64]{1,0:T(8,128)(2,1)} %rope_ref.1) | copy-start | bytes 3076
